TPU v7x, 256 devices: a whole 4x4x8 slice. The times are simulated.
256 devices in a mesh: dp: 32 (over x, z_hi, core), seq: 8 (over z_lo, y).
Axes of the slice: x: 4, y: 4, z: 8 (z_hi: 4, z_lo: 2; z = z_hi * 2 + z_lo), core: 2. Of those that a mesh axis runs over, the one named last changes fastest.
Arguments:
- query_rows: bfloat16 [32768, 1536], P(('dp', 'seq')), may hold values from -6 to 6
- key_rows: bfloat16 [32768, 1536], P(('dp', 'seq')), may hold values from -6 to 6
- value_rows: bfloat16 [32768, 1536], P(('dp', 'seq')), may hold values from -6 to 6
- d_caption: bfloat16 [4096, 1536], P(('dp', 'seq')), may hold values from -6 to 6
- d_image: bfloat16 [28672, 1536], P(('dp', 'seq')), may hold values from -6 to 6
- proj_weight: bfloat16 [1536, 1536], P(('dp', 'seq')), may hold values from -0.15625 to 0.15625
- lengths: int32 [32], P('dp'), may hold values from 224 to 896, as said below
Outputs:
- grad_query: bfloat16 [32768, 1536], P(('dp', 'seq'))
- grad_key: bfloat16 [32768, 1536], P(('dp', 'seq'))
- grad_value: bfloat16 [32768, 1536], P(('dp', 'seq'))
- grad_proj: float32 [1536, 1536], P(('dp', 'seq'))
Inputs may be any that keep to these rules, and one draw needn't show every extreme that they name: `lengths`: one sequence has exactly 896 image tokens.
All inputs are finite; a program needn't handle non-finite values.
Results may differ from a plain program's by a relative error of at most 0.019.
Values may be sent and summed in bfloat16 or wider, within the bound.
A program may use at most 64 MiB of HBM per device.

v0:
```python
import jax
import jax.numpy as jnp
from jax import lax
from jax.sharding import PartitionSpec as P

HEADS = 12
HD = 128
CAP_DEV = 16
IMG_DEV = 112


def token_valid(positions, length):
    per_device = CAP_DEV + IMG_DEV
    block = positions // per_device
    offset = positions % per_device
    image_index = block * IMG_DEV + offset - CAP_DEV
    return jnp.logical_or(offset < CAP_DEV, image_index < length)


def block_terms(query_blk, grad_blk, keyset, valueset, valid_keys, scale):
    scores = (
        lax.dot_general(
            query_blk, keyset, (((1,), (1,)), ((), ())), preferred_element_type=jnp.float32
        )
        * scale
    )
    scores = jnp.where(valid_keys[None, :], scores, -jnp.inf)
    top = jnp.max(scores, axis=-1, keepdims=True)
    expo = jnp.exp(scores - top)
    probs = expo / jnp.sum(expo, axis=-1, keepdims=True)
    probs_low = probs.astype(jnp.bfloat16)
    attn = jnp.dot(probs_low, valueset, preferred_element_type=jnp.float32).astype(jnp.bfloat16)
    delta = jnp.sum(grad_blk.astype(jnp.float32) * attn.astype(jnp.float32), axis=-1)
    dprob = lax.dot_general(
        grad_blk, valueset, (((1,), (1,)), ((), ())), preferred_element_type=jnp.float32
    )
    dscore = (probs * (dprob - delta[:, None])).astype(jnp.bfloat16)
    grad_q = (jnp.dot(dscore, keyset, preferred_element_type=jnp.float32) * scale).astype(
        jnp.bfloat16
    )
    part_k = (
        lax.dot_general(
            dscore, query_blk, (((0,), (0,)), ((), ())), preferred_element_type=jnp.float32
        )
        * scale
    )
    part_v = lax.dot_general(
        probs_low, grad_blk, (((0,), (0,)), ((), ())), preferred_element_type=jnp.float32
    )
    return (attn, grad_q, part_k, part_v)


def columns(array, start):
    return lax.dynamic_slice_in_dim(array, start, HD, 1)


def shards(query_rows, key_rows, value_rows, d_caption, d_image, proj_weight, lengths):
    groups = lax.axis_size("seq")
    here = lax.axis_index("seq")
    per_device = CAP_DEV + IMG_DEV
    length = lengths[0]
    scale = HD ** (-0.5)
    width = HEADS * HD
    image_do = lax.dot_general(
        d_image,
        lax.all_gather(proj_weight, ("dp", "seq"), axis=0, tiled=True),
        (((1,), (1,)), ((), ())),
        preferred_element_type=jnp.float32,
    ).astype(jnp.bfloat16)
    local_pos = here * per_device + jnp.arange(per_device, dtype=jnp.int32)
    valid_local = token_valid(local_pos, length)
    grad_out = jnp.concatenate([d_caption, image_do], axis=0)
    grad_out = jnp.where(valid_local[:, None], grad_out, jnp.zeros_like(grad_out))
    span = groups * per_device
    valid_keys = token_valid(jnp.arange(span, dtype=jnp.int32), length)
    keys_all, values_all = (
        lax.all_gather(key_rows, "seq", axis=0, tiled=True),
        lax.all_gather(value_rows, "seq", axis=0, tiled=True),
    )

    def head_step(carry, head):
        attn_acc, gq_acc, part_acc = carry
        start = head * HD
        attn, grad_q, part_k, part_v = block_terms(
            columns(query_rows, start),
            columns(grad_out, start),
            columns(keys_all, start),
            columns(values_all, start),
            valid_keys,
            scale,
        )
        attn_acc = lax.dynamic_update_slice_in_dim(attn_acc, attn, start, 1)
        gq_acc = lax.dynamic_update_slice_in_dim(gq_acc, grad_q, start, 1)
        part_acc = lax.dynamic_update_slice_in_dim(part_acc, part_k, start, 1)
        part_acc = lax.dynamic_update_slice_in_dim(part_acc, part_v, width + start, 1)
        return ((attn_acc, gq_acc, part_acc), None)

    start_rows = jnp.zeros((per_device, width), jnp.bfloat16)
    start_parts = jnp.zeros((span, 2 * width), jnp.float32)
    (attn_flat, grad_query, partials), unused = lax.scan(
        head_step, (start_rows, start_rows, start_parts), jnp.arange(HEADS, dtype=jnp.int32)
    )
    summed = lax.psum_scatter(
        partials.astype(jnp.bfloat16), "seq", scatter_dimension=0, tiled=True
    ).astype(jnp.float32)
    grad_key = summed[:, :width].astype(jnp.bfloat16)
    grad_value = summed[:, width:].astype(jnp.bfloat16)
    outs_img = jnp.where(
        valid_local[CAP_DEV:, None], attn_flat[CAP_DEV:], jnp.zeros_like(attn_flat[CAP_DEV:])
    )
    term = lax.dot_general(
        outs_img, d_image, (((0,), (0,)), ((), ())), preferred_element_type=jnp.float32
    )
    grad_proj = lax.psum_scatter(term, ("dp", "seq"), scatter_dimension=0, tiled=True)
    return (grad_query, grad_key, grad_value, grad_proj)


def solution(mesh):
    placed = (
        P(("dp", "seq"), None),
        P(("dp", "seq"), None),
        P(("dp", "seq"), None),
        P(("dp", "seq"), None),
        P(("dp", "seq"), None),
        P(("dp", "seq"), None),
        P("dp"),
    )
    return jax.shard_map(
        shards,
        mesh=mesh,
        in_specs=placed,
        out_specs=(
            P(("dp", "seq"), None),
            P(("dp", "seq"), None),
            P(("dp", "seq"), None),
            P(("dp", "seq"), None),
        ),
        check_vma=False,
    )
```

profile of v0, /device:TPU:4, one launch (start us, length us, event | category | flops | bytes accessed | tf_op | source)
XLA Modules:
  0.0 2246.9 jit_solution(15719862227060899639)
XLA Ops:
  10.1 712.2 %all-gather.9.cloned.1.call-done = bf16[256,6,1536]{2,1,0:T(8,128)(2,1)} async-done(((bf16[1,6,1536]{2,1,0:T(8,128)(2,1)}), bf16[256,6,1536]{2,1,0:T(8,128)(2,1)}) %all-gather.9.cloned.1.call-update) | async-done | bytes 4718608 | tf_op jit(solution)/shard_map/all_gather | solution.py:66
  722.4 8.4 reshape.52
  734.8 40.9 %all-gather.5.cloned.1.call-done = bf16[1024,1536]{1,0:T(8,128)(2,1)} async-done(((bf16[128,1536]{1,0:T(8,128)(2,1)}), bf16[1024,1536]{1,0:T(8,128)(2,1)}) %all-gather.5.cloned.1.call-update) | async-done | bytes 3145744 | tf_op jit(solution)/shard_map/all_gather | solution.py:77
  775.7 48.3 %all-gather.7.cloned.1.call-done = bf16[1024,1536]{1,0:T(8,128)(2,1)} async-done(((bf16[128,1536]{1,0:T(8,128)(2,1)}), bf16[1024,1536]{1,0:T(8,128)(2,1)}) %all-gather.7.cloned.1.call-update) | async-done | bytes 3145744 | tf_op jit(solution)/shard_map/all_gather | solution.py:78
  827.5 122.5 %while.17 = (s32[]{:T(128)}, bf16[128,1536]{0,1:T(8,128)(2,1)S(1)}, bf16[128,1536]{1,0:T(8,128)(2,1)S(1)}, bf16[1024,3072]{1,0:T(8,128)(2,1)}, s32[12]{0:T(128)S...) while((s32[]{:T(128)}, bf16[128,1536]{0,1:T(8,128)(2,1)S(1)}, ...), condition=%wide.region_4.5_spmd.clone, body=%wide.region_0.4_spmd.clone.sunk | while | flops 203687552 | bytes 5942050 | solution.py:100
  950.1 5.1 fusion.37
  955.1 643.5 %fusion.2 = f32[8,1536]{1,0:T(8,128)S(1)} fusion(f32[1536,1536]{1,0:T(8,128)} %fusion.37), kind=kCustom, calls=%all-reduce-scatter | all-reduce-scatter fusion | flops 3145729 | bytes 9486336
  1598.6 84.5 %collective-permute-start = (f32[8,1536]{1,0:T(8,128)S(1)}, f32[8,1536]{1,0:T(8,128)S(1)}, u32[]{:S(2)}, u32[]{:S(2)}) collective-permute-start(f32[8,1536]{1,0:T(8,128)S(1)} %fusion.2), channel_id=1, source_target_pairs={{0,1},{1,2},{2,3},{3,4},{4,5},{5,6},{6,7},{7,8},{8,9},{9,10},{10,1... | collective-permute-start | bytes 147464
  1683.1 13.2 collective-permute-start.1
  1696.4 13.1 collective-permute-start.10
  1712.6 13.1 collective-permute-start.11
  1725.8 13.1 collective-permute-start.12
  1738.9 13.1 collective-permute-start.13
  1752.1 13.1 collective-permute-start.14
  1765.2 13.1 collective-permute-start.15
  1778.4 13.1 collective-permute-start.16
  1791.5 13.1 collective-permute-start.17
  1804.7 13.1 collective-permute-start.18
  1817.8 13.1 collective-permute-start.19
  1831.0 13.1 collective-permute-start.2
  1844.1 13.1 collective-permute-start.20
  1857.3 13.1 collective-permute-start.21
  1870.4 13.1 collective-permute-start.22
  1883.6 13.1 collective-permute-start.23
  1896.7 13.1 collective-permute-start.24
  1909.9 13.1 collective-permute-start.25
  1923.0 13.1 collective-permute-start.26
  1936.2 13.1 collective-permute-start.27
  1949.3 6.6 collective-permute-start.28
  1955.9 7.4 collective-permute-start.29
  1963.3 10.2 collective-permute-start.3
  1973.5 7.9 collective-permute-start.30
  1981.5 5.7 collective-permute-start.31
  1987.1 5.9 collective-permute-start.32
  2011.6 15.0 collective-permute-start.4
  2026.7 9.0 collective-permute-start.40
  2035.7 4.8 collective-permute-start.41
  2040.5 5.8 collective-permute-start.42
  2062.3 14.2 collective-permute-start.5
  2076.5 9.3 collective-permute-start.50
  2106.6 12.6 collective-permute-start.6
  2119.1 7.1 collective-permute-start.60
  2126.2 5.0 collective-permute-start.61
  2133.2 8.7 collective-permute-start.7
  2141.9 13.1 collective-permute-start.8
  2155.0 13.3 collective-permute-start.9
  2170.0 7.8 collective-permute-done.9
  2177.8 59.9 %concatenate.4 = f32[518,1536]{1,0:T(8,128)S(1)} concatenate(f32[6,1536]{1,0:T(8,128)} %copy-done.6, f32[8,1536]{1,0:T(8,128)} %copy-done.42, f32[8,1536]{1,0:T(8,128)} %copy-done.41, f32[8,1536]{1,0:T(8,128)} %collective-permute-done.60, f32[8,1536]{1,0:T(8,128)} %collective-permute-done.59, f32[8,1536]{1,0:T(8,128)} %collective-permute-done.58, ...), dimensions={0} | concatenate | bytes 6365184
  (344 shorter events, 187.5 us)
Async XLA Ops:
  7.2 715.2 %all-gather.9.cloned.1.call-start = ((), (), s32[]{:S(2)}) async-start(), calls=%async_computation.4 | async-start | bytes 6316032 | tf_op jit(solution)/shard_map/all_gather | solution.py:66
  7.9 767.8 %all-gather.5.cloned.1.call-start = ((), (), s32[]{:S(2)}) async-start(), calls=%async_computation.1 | async-start | bytes 3538944 | tf_op jit(solution)/shard_map/all_gather | solution.py:77
  8.7 815.3 %all-gather.7.cloned.1.call-start = ((), (), s32[]{:S(2)}) async-start(), calls=%async_computation.2 | async-start | bytes 3538944 | tf_op jit(solution)/shard_map/all_gather | solution.py:78
  9.4 2228.9 %reduce-scatter.4.cloned.1.call-start = ((), (), s32[]{:S(2)}) async-start(), calls=%async_computation.3 | async-start | bytes 7077888 | tf_op jit(solution)/shard_map/reduce_scatter | solution.py:103
  1598.6 140.3 %collective-permute-start = (f32[8,1536]{1,0:T(8,128)S(1)}, f32[8,1536]{1,0:T(8,128)S(1)}, u32[]{:S(2)}, u32[]{:S(2)}) collective-permute-start(f32[8,1536]{1,0:T(8,128)S(1)} %fusion.2), channel_id=1, source_target_pairs={{0,1},{1,2},{2,3},{3,4},{4,5},{5,6},{6,7},{7,8},{8,9},{9,10},{10,1... | collective-permute-start | bytes 147464
  1683.1 68.9 %collective-permute-start.1 = (f32[8,1536]{1,0:T(8,128)S(1)}, f32[8,1536]{1,0:T(8,128)S(1)}, u32[]{:S(2)}, u32[]{:S(2)}) collective-permute-start(f32[8,1536]{1,0:T(8,128)S(1)} %fusion.2), channel_id=1, source_target_pairs={{0,2},{1,3},{2,4},{3,5},{4,6},{5,7},{6,8},{7,9},{8,10},{9,11},{10,... | collective-permute-start | bytes 147464
  1696.4 68.8 %collective-permute-start.10 = (f32[8,1536]{1,0:T(8,128)S(1)}, f32[8,1536]{1,0:T(8,128)S(1)}, u32[]{:S(2)}, u32[]{:S(2)}) collective-permute-start(f32[8,1536]{1,0:T(8,128)S(1)} %fusion.2), channel_id=1, source_target_pairs={{0,11},{1,12},{2,13},{3,14},{4,15},{5,16},{6,17},{7,18},{8,19},{9,... | collective-permute-start | bytes 147464
  1712.6 65.8 %collective-permute-start.11 = (f32[8,1536]{1,0:T(8,128)S(1)}, f32[8,1536]{1,0:T(8,128)S(1)}, u32[]{:S(2)}, u32[]{:S(2)}) collective-permute-start(f32[8,1536]{1,0:T(8,128)S(1)} %fusion.2), channel_id=1, source_target_pairs={{0,12},{1,13},{2,14},{3,15},{4,16},{5,17},{6,18},{7,19},{8,20},{9,... | collective-permute-start | bytes 147464
  1725.8 65.7 %collective-permute-start.12 = (f32[8,1536]{1,0:T(8,128)S(1)}, f32[8,1536]{1,0:T(8,128)S(1)}, u32[]{:S(2)}, u32[]{:S(2)}) collective-permute-start(f32[8,1536]{1,0:T(8,128)S(1)} %fusion.2), channel_id=1, source_target_pairs={{0,13},{1,14},{2,15},{3,16},{4,17},{5,18},{6,19},{7,20},{8,21},{9,... | collective-permute-start | bytes 147464
  1738.9 65.7 %collective-permute-start.13 = (f32[8,1536]{1,0:T(8,128)S(1)}, f32[8,1536]{1,0:T(8,128)S(1)}, u32[]{:S(2)}, u32[]{:S(2)}) collective-permute-start(f32[8,1536]{1,0:T(8,128)S(1)} %fusion.2), channel_id=1, source_target_pairs={{0,14},{1,15},{2,16},{3,17},{4,18},{5,19},{6,20},{7,21},{8,22},{9,... | collective-permute-start | bytes 147464
  1752.1 65.7 %collective-permute-start.14 = (f32[8,1536]{1,0:T(8,128)S(1)}, f32[8,1536]{1,0:T(8,128)S(1)}, u32[]{:S(2)}, u32[]{:S(2)}) collective-permute-start(f32[8,1536]{1,0:T(8,128)S(1)} %fusion.2), channel_id=1, source_target_pairs={{0,15},{1,16},{2,17},{3,18},{4,19},{5,20},{6,21},{7,22},{8,23},{9,... | collective-permute-start | bytes 147464
  1765.2 65.7 %collective-permute-start.15 = (f32[8,1536]{1,0:T(8,128)S(1)}, f32[8,1536]{1,0:T(8,128)S(1)}, u32[]{:S(2)}, u32[]{:S(2)}) collective-permute-start(f32[8,1536]{1,0:T(8,128)S(1)} %fusion.2), channel_id=1, source_target_pairs={{0,16},{1,17},{2,18},{3,19},{4,20},{5,21},{6,22},{7,23},{8,24},{9,... | collective-permute-start | bytes 147464
  1778.4 65.7 %collective-permute-start.16 = (f32[8,1536]{1,0:T(8,128)S(1)}, f32[8,1536]{1,0:T(8,128)S(1)}, u32[]{:S(2)}, u32[]{:S(2)}) collective-permute-start(f32[8,1536]{1,0:T(8,128)S(1)} %fusion.2), channel_id=1, source_target_pairs={{0,17},{1,18},{2,19},{3,20},{4,21},{5,22},{6,23},{7,24},{8,25},{9,... | collective-permute-start | bytes 147464
  1791.5 65.7 %collective-permute-start.17 = (f32[8,1536]{1,0:T(8,128)S(1)}, f32[8,1536]{1,0:T(8,128)S(1)}, u32[]{:S(2)}, u32[]{:S(2)}) collective-permute-start(f32[8,1536]{1,0:T(8,128)S(1)} %fusion.2), channel_id=1, source_target_pairs={{0,18},{1,19},{2,20},{3,21},{4,22},{5,23},{6,24},{7,25},{8,26},{9,... | collective-permute-start | bytes 147464
  1804.7 65.7 %collective-permute-start.18 = (f32[8,1536]{1,0:T(8,128)S(1)}, f32[8,1536]{1,0:T(8,128)S(1)}, u32[]{:S(2)}, u32[]{:S(2)}) collective-permute-start(f32[8,1536]{1,0:T(8,128)S(1)} %fusion.2), channel_id=1, source_target_pairs={{0,19},{1,20},{2,21},{3,22},{4,23},{5,24},{6,25},{7,26},{8,27},{9,... | collective-permute-start | bytes 147464
  1817.8 65.7 %collective-permute-start.19 = (f32[8,1536]{1,0:T(8,128)S(1)}, f32[8,1536]{1,0:T(8,128)S(1)}, u32[]{:S(2)}, u32[]{:S(2)}) collective-permute-start(f32[8,1536]{1,0:T(8,128)S(1)} %fusion.2), channel_id=1, source_target_pairs={{0,20},{1,21},{2,22},{3,23},{4,24},{5,25},{6,26},{7,27},{8,28},{9,... | collective-permute-start | bytes 147464
  1831.0 65.7 %collective-permute-start.2 = (f32[8,1536]{1,0:T(8,128)S(1)}, f32[8,1536]{1,0:T(8,128)S(1)}, u32[]{:S(2)}, u32[]{:S(2)}) collective-permute-start(f32[8,1536]{1,0:T(8,128)S(1)} %fusion.2), channel_id=1, source_target_pairs={{0,3},{1,4},{2,5},{3,6},{4,7},{5,8},{6,9},{7,10},{8,11},{9,12},{10... | collective-permute-start | bytes 147464
  1844.1 65.7 %collective-permute-start.20 = (f32[8,1536]{1,0:T(8,128)S(1)}, f32[8,1536]{1,0:T(8,128)S(1)}, u32[]{:S(2)}, u32[]{:S(2)}) collective-permute-start(f32[8,1536]{1,0:T(8,128)S(1)} %fusion.2), channel_id=1, source_target_pairs={{0,21},{1,22},{2,23},{3,24},{4,25},{5,26},{6,27},{7,28},{8,29},{9,... | collective-permute-start | bytes 147464
  1857.3 65.7 %collective-permute-start.21 = (f32[8,1536]{1,0:T(8,128)S(1)}, f32[8,1536]{1,0:T(8,128)S(1)}, u32[]{:S(2)}, u32[]{:S(2)}) collective-permute-start(f32[8,1536]{1,0:T(8,128)S(1)} %fusion.2), channel_id=1, source_target_pairs={{0,22},{1,23},{2,24},{3,25},{4,26},{5,27},{6,28},{7,29},{8,30},{9,... | collective-permute-start | bytes 147464
  1870.4 65.7 %collective-permute-start.22 = (f32[8,1536]{1,0:T(8,128)S(1)}, f32[8,1536]{1,0:T(8,128)S(1)}, u32[]{:S(2)}, u32[]{:S(2)}) collective-permute-start(f32[8,1536]{1,0:T(8,128)S(1)} %fusion.2), channel_id=1, source_target_pairs={{0,23},{1,24},{2,25},{3,26},{4,27},{5,28},{6,29},{7,30},{8,31},{9,... | collective-permute-start | bytes 147464
  1883.6 65.7 %collective-permute-start.23 = (f32[8,1536]{1,0:T(8,128)S(1)}, f32[8,1536]{1,0:T(8,128)S(1)}, u32[]{:S(2)}, u32[]{:S(2)}) collective-permute-start(f32[8,1536]{1,0:T(8,128)S(1)} %fusion.2), channel_id=1, source_target_pairs={{0,24},{1,25},{2,26},{3,27},{4,28},{5,29},{6,30},{7,31},{8,32},{9,... | collective-permute-start | bytes 147464
  1896.7 59.2 %collective-permute-start.24 = (f32[8,1536]{1,0:T(8,128)S(1)}, f32[8,1536]{1,0:T(8,128)S(1)}, u32[]{:S(2)}, u32[]{:S(2)}) collective-permute-start(f32[8,1536]{1,0:T(8,128)S(1)} %fusion.2), channel_id=1, source_target_pairs={{0,25},{1,26},{2,27},{3,28},{4,29},{5,30},{6,31},{7,32},{8,33},{9,... | collective-permute-start | bytes 147464
  1909.9 53.4 %collective-permute-start.25 = (f32[8,1536]{1,0:T(8,128)S(1)}, f32[8,1536]{1,0:T(8,128)S(1)}, u32[]{:S(2)}, u32[]{:S(2)}) collective-permute-start(f32[8,1536]{1,0:T(8,128)S(1)} %fusion.2), channel_id=1, source_target_pairs={{0,26},{1,27},{2,28},{3,29},{4,30},{5,31},{6,32},{7,33},{8,34},{9,... | collective-permute-start | bytes 147464
  1923.0 50.5 %collective-permute-start.26 = (f32[8,1536]{1,0:T(8,128)S(1)}, f32[8,1536]{1,0:T(8,128)S(1)}, u32[]{:S(2)}, u32[]{:S(2)}) collective-permute-start(f32[8,1536]{1,0:T(8,128)S(1)} %fusion.2), channel_id=1, source_target_pairs={{0,27},{1,28},{2,29},{3,30},{4,31},{5,32},{6,33},{7,34},{8,35},{9,... | collective-permute-start | bytes 147464
  1936.2 45.3 %collective-permute-start.27 = (f32[8,1536]{1,0:T(8,128)S(1)}, f32[8,1536]{1,0:T(8,128)S(1)}, u32[]{:S(2)}, u32[]{:S(2)}) collective-permute-start(f32[8,1536]{1,0:T(8,128)S(1)} %fusion.2), channel_id=1, source_target_pairs={{0,28},{1,29},{2,30},{3,31},{4,32},{5,33},{6,34},{7,35},{8,36},{9,... | collective-permute-start | bytes 147464
  1949.3 37.8 %collective-permute-start.28 = (f32[8,1536]{1,0:T(8,128)S(1)}, f32[8,1536]{1,0:T(8,128)S(1)}, u32[]{:S(2)}, u32[]{:S(2)}) collective-permute-start(f32[8,1536]{1,0:T(8,128)S(1)} %fusion.2), channel_id=1, source_target_pairs={{0,29},{1,30},{2,31},{3,32},{4,33},{5,34},{6,35},{7,36},{8,37},{9,... | collective-permute-start | bytes 147464
  1955.9 37.2 %collective-permute-start.29 = (f32[8,1536]{1,0:T(8,128)S(1)}, f32[8,1536]{1,0:T(8,128)S(1)}, u32[]{:S(2)}, u32[]{:S(2)}) collective-permute-start(f32[8,1536]{1,0:T(8,128)S(1)} %fusion.2), channel_id=1, source_target_pairs={{0,30},{1,31},{2,32},{3,33},{4,34},{5,35},{6,36},{7,37},{8,38},{9,... | collective-permute-start | bytes 147464
  1963.3 34.3 %collective-permute-start.3 = (f32[8,1536]{1,0:T(8,128)S(1)}, f32[8,1536]{1,0:T(8,128)S(1)}, u32[]{:S(2)}, u32[]{:S(2)}) collective-permute-start(f32[8,1536]{1,0:T(8,128)S(1)} %fusion.2), channel_id=1, source_target_pairs={{0,4},{1,5},{2,6},{3,7},{4,8},{5,9},{6,10},{7,11},{8,12},{9,13},{1... | collective-permute-start | bytes 147464
  1973.5 26.1 %collective-permute-start.30 = (f32[8,1536]{1,0:T(8,128)S(1)}, f32[8,1536]{1,0:T(8,128)S(1)}, u32[]{:S(2)}, u32[]{:S(2)}) collective-permute-start(f32[8,1536]{1,0:T(8,128)S(1)} %fusion.2), channel_id=1, source_target_pairs={{0,31},{1,32},{2,33},{3,34},{4,35},{5,36},{6,37},{7,38},{8,39},{9,... | collective-permute-start | bytes 147464
  2001.6 25.1 %collective-permute-start.36 = (f32[8,1536]{1,0:T(8,128)S(1)}, f32[8,1536]{1,0:T(8,128)S(1)}, u32[]{:S(2)}, u32[]{:S(2)}) collective-permute-start(f32[8,1536]{1,0:T(8,128)S(1)} %fusion.2), channel_id=1, source_target_pairs={{0,37},{1,38},{2,39},{3,40},{4,41},{5,42},{6,43},{7,44},{8,45},{9,... | collective-permute-start | bytes 147464
  2003.5 32.1 %collective-permute-start.37 = (f32[8,1536]{1,0:T(8,128)S(1)}, f32[8,1536]{1,0:T(8,128)S(1)}, u32[]{:S(2)}, u32[]{:S(2)}) collective-permute-start(f32[8,1536]{1,0:T(8,128)S(1)} %fusion.2), channel_id=1, source_target_pairs={{0,38},{1,39},{2,40},{3,41},{4,42},{5,43},{6,44},{7,45},{8,46},{9,... | collective-permute-start | bytes 147464
  2005.5 35.0 %collective-permute-start.38 = (f32[8,1536]{1,0:T(8,128)S(1)}, f32[8,1536]{1,0:T(8,128)S(1)}, u32[]{:S(2)}, u32[]{:S(2)}) collective-permute-start(f32[8,1536]{1,0:T(8,128)S(1)} %fusion.2), channel_id=1, source_target_pairs={{0,39},{1,40},{2,41},{3,42},{4,43},{5,44},{6,45},{7,46},{8,47},{9,... | collective-permute-start | bytes 147464
  2009.4 36.9 %collective-permute-start.39 = (f32[8,1536]{1,0:T(8,128)S(1)}, f32[8,1536]{1,0:T(8,128)S(1)}, u32[]{:S(2)}, u32[]{:S(2)}) collective-permute-start(f32[8,1536]{1,0:T(8,128)S(1)} %fusion.2), channel_id=1, source_target_pairs={{0,40},{1,41},{2,42},{3,43},{4,44},{5,45},{6,46},{7,47},{8,48},{9,... | collective-permute-start | bytes 147464
  2011.6 36.6 %collective-permute-start.4 = (f32[8,1536]{1,0:T(8,128)S(1)}, f32[8,1536]{1,0:T(8,128)S(1)}, u32[]{:S(2)}, u32[]{:S(2)}) collective-permute-start(f32[8,1536]{1,0:T(8,128)S(1)} %fusion.2), channel_id=1, source_target_pairs={{0,5},{1,6},{2,7},{3,8},{4,9},{5,10},{6,11},{7,12},{8,13},{9,14},{... | collective-permute-start | bytes 147464
  2052.2 24.3 %collective-permute-start.46 = (f32[8,1536]{1,0:T(8,128)S(1)}, f32[8,1536]{1,0:T(8,128)}, u32[]{:S(2)}, u32[]{:S(2)}) collective-permute-start(f32[8,1536]{1,0:T(8,128)S(1)} %fusion.2), channel_id=1, source_target_pairs={{0,47},{1,48},{2,49},{3,50},{4,51},{5,52},{6,53},{7,54},{8,55},{9,... | collective-permute-start | bytes 147464
  2054.1 31.7 %collective-permute-start.47 = (f32[8,1536]{1,0:T(8,128)S(1)}, f32[8,1536]{1,0:T(8,128)}, u32[]{:S(2)}, u32[]{:S(2)}) collective-permute-start(f32[8,1536]{1,0:T(8,128)S(1)} %fusion.2), channel_id=1, source_target_pairs={{0,48},{1,49},{2,50},{3,51},{4,52},{5,53},{6,54},{7,55},{8,56},{9,... | collective-permute-start | bytes 147464
  2057.2 32.4 %collective-permute-start.48 = (f32[8,1536]{1,0:T(8,128)S(1)}, f32[8,1536]{1,0:T(8,128)}, u32[]{:S(2)}, u32[]{:S(2)}) collective-permute-start(f32[8,1536]{1,0:T(8,128)S(1)} %fusion.2), channel_id=1, source_target_pairs={{0,49},{1,50},{2,51},{3,52},{4,53},{5,54},{6,55},{7,56},{8,57},{9,... | collective-permute-start | bytes 147464
  2059.1 32.4 %collective-permute-start.49 = (f32[8,1536]{1,0:T(8,128)S(1)}, f32[8,1536]{1,0:T(8,128)}, u32[]{:S(2)}, u32[]{:S(2)}) collective-permute-start(f32[8,1536]{1,0:T(8,128)S(1)} %fusion.2), channel_id=1, source_target_pairs={{0,50},{1,51},{2,52},{3,53},{4,54},{5,55},{6,56},{7,57},{8,58},{9,... | collective-permute-start | bytes 147464
  2062.3 31.7 %collective-permute-start.5 = (f32[8,1536]{1,0:T(8,128)S(1)}, f32[8,1536]{1,0:T(8,128)}, u32[]{:S(2)}, u32[]{:S(2)}) collective-permute-start(f32[8,1536]{1,0:T(8,128)S(1)} %fusion.2), channel_id=1, source_target_pairs={{0,6},{1,7},{2,8},{3,9},{4,10},{5,11},{6,12},{7,13},{8,14},{9,15},... | collective-permute-start | bytes 147464
  2099.9 26.3 %collective-permute-start.57 = (f32[8,1536]{1,0:T(8,128)S(1)}, f32[8,1536]{1,0:T(8,128)}, u32[]{:S(2)}, u32[]{:S(2)}) collective-permute-start(f32[8,1536]{1,0:T(8,128)S(1)} %fusion.2), channel_id=1, source_target_pairs={{0,58},{1,59},{2,60},{3,61},{4,62},{5,63},{6,64},{7,65},{8,66},{9,... | collective-permute-start | bytes 147464
  2102.0 29.3 %collective-permute-start.58 = (f32[8,1536]{1,0:T(8,128)S(1)}, f32[8,1536]{1,0:T(8,128)}, u32[]{:S(2)}, u32[]{:S(2)}) collective-permute-start(f32[8,1536]{1,0:T(8,128)S(1)} %fusion.2), channel_id=1, source_target_pairs={{0,59},{1,60},{2,61},{3,62},{4,63},{5,64},{6,65},{7,66},{8,67},{9,... | collective-permute-start | bytes 147464
  2104.6 28.6 %collective-permute-start.59 = (f32[8,1536]{1,0:T(8,128)S(1)}, f32[8,1536]{1,0:T(8,128)}, u32[]{:S(2)}, u32[]{:S(2)}) collective-permute-start(f32[8,1536]{1,0:T(8,128)S(1)} %fusion.2), channel_id=1, source_target_pairs={{0,60},{1,61},{2,62},{3,63},{4,64},{5,65},{6,66},{7,67},{8,68},{9,... | collective-permute-start | bytes 147464
  2106.6 35.3 %collective-permute-start.6 = (f32[8,1536]{1,0:T(8,128)S(1)}, f32[8,1536]{1,0:T(8,128)}, u32[]{:S(2)}, u32[]{:S(2)}) collective-permute-start(f32[8,1536]{1,0:T(8,128)S(1)} %fusion.2), channel_id=1, source_target_pairs={{0,7},{1,8},{2,9},{3,10},{4,11},{5,12},{6,13},{7,14},{8,15},{9,16}... | collective-permute-start | bytes 147464
  2119.1 35.9 %collective-permute-start.60 = (f32[8,1536]{1,0:T(8,128)S(1)}, f32[8,1536]{1,0:T(8,128)}, u32[]{:S(2)}, u32[]{:S(2)}) collective-permute-start(f32[8,1536]{1,0:T(8,128)S(1)} %fusion.2), channel_id=1, source_target_pairs={{0,61},{1,62},{2,63},{3,64},{4,65},{5,66},{6,67},{7,68},{8,69},{9,... | collective-permute-start | bytes 147464
  2126.2 42.5 %collective-permute-start.61 = (f32[8,1536]{1,0:T(8,128)S(1)}, f32[8,1536]{1,0:T(8,128)S(1)}, u32[]{:S(2)}, u32[]{:S(2)}) collective-permute-start(f32[8,1536]{1,0:T(8,128)S(1)} %fusion.2), channel_id=1, source_target_pairs={{0,62},{1,63},{2,64},{3,65},{4,66},{5,67},{6,68},{7,69},{8,70},{9,... | collective-permute-start | bytes 147464
  2131.3 37.5 %collective-permute-start.62 = (f32[8,1536]{1,0:T(8,128)S(1)}, f32[8,1536]{1,0:T(8,128)S(1)}, u32[]{:S(2)}, u32[]{:S(2)}) collective-permute-start(f32[8,1536]{1,0:T(8,128)S(1)} %fusion.2), channel_id=1, source_target_pairs={{0,63},{1,64},{2,65},{3,66},{4,67},{5,68},{6,69},{7,70},{8,71},{9,... | collective-permute-start | bytes 147464
  2133.2 35.6 %collective-permute-start.7 = (f32[8,1536]{1,0:T(8,128)S(1)}, f32[8,1536]{1,0:T(8,128)S(1)}, u32[]{:S(2)}, u32[]{:S(2)}) collective-permute-start(f32[8,1536]{1,0:T(8,128)S(1)} %fusion.2), channel_id=1, source_target_pairs={{0,8},{1,9},{2,10},{3,11},{4,12},{5,13},{6,14},{7,15},{8,16},{9,17... | collective-permute-start | bytes 147464
  2141.9 26.9 %collective-permute-start.8 = (f32[8,1536]{1,0:T(8,128)S(1)}, f32[8,1536]{1,0:T(8,128)S(1)}, u32[]{:S(2)}, u32[]{:S(2)}) collective-permute-start(f32[8,1536]{1,0:T(8,128)S(1)} %fusion.2), channel_id=1, source_target_pairs={{0,9},{1,10},{2,11},{3,12},{4,13},{5,14},{6,15},{7,16},{8,17},{9,1... | collective-permute-start | bytes 147464
  (66 other events, 11451.0 us)
Sparse Core Ops, SparseCore 0:
  9.9 712.4 all-gather.8
  724.1 51.5 all-gather.4
  777.5 46.4 all-gather.6
  950.1 85.7 reduce-scatter.3
where the time goes:
time: 2260 us; the launch traced here: 2250 us
  waiting for transfers between devices  814 us (36%)
  blocking collectives  643 us (28%)
  starting transfers between devices  566 us (25%)
  matrix products  103 us (5%)
  local copies, waits for them, and re-layouts  84.5 us (4%)
    all_gather x1, waiting for transfers between devices, shards(): lax.all_gather(proj_weight, ('dp', 'seq'), axis=0, tiled=True)  712 us
    unnamed x1, blocking collectives  643 us
    unnamed x64, starting transfers between devices  566 us
    unnamed x96, local copies, waits for them, and re-layouts  70.4 us
    all_gather x1, waiting for transfers between devices, shards(): lax.all_gather(value_rows, 'seq', axis=0, tiled=True)  48.3 us
  transfers between devices with their start and end apart: 68, of which 6 were waited for; matrix products, arithmetic and copies ran while one was open for 32% of the time, Pallas kernels for 0%

commit v1 on v0

v1 whole, which is shorter than its diff:
```python
import jax
import jax.numpy as jnp
from jax import lax
from jax.experimental import pallas as pl
from jax.experimental.pallas import tpu as pltpu
from jax.sharding import PartitionSpec as P

MESH = pl.DeviceIdType.MESH
F32, BF = jnp.float32, jnp.bfloat16
SCALE = 128 ** (-0.5)
LOG2E = 1.4426950408889634
NEG = -1e30
NT = (((1,), (1,)), ((), ()))
TT = (((0,), (0,)), ((), ()))
NN = (((1,), (0,)), ((), ()))


def dot(a, b, dims):
    return lax.dot_general(a, b, dims, preferred_element_type=F32)


def device(x, y, z, c):
    return ((x * 4 + z // 2) * 2 + c, (z % 2) * 4 + y)


def select_rows(half):
    row = lax.broadcasted_iota(jnp.int32, (256, 384), 0)
    col = lax.broadcasted_iota(jnp.int32, (256, 384), 1)
    place, z = row % 32, row // 32
    r, source = place % 8, place // 8
    feature = 48 * ((z // 2) * 2 + half) + 6 * ((z % 2) * 4 + source) + r
    return jnp.where((feature == col) & (r < 6), 1.0, 0.0).astype(BF)


def kernel(
    len_ref, q_ref, k_ref, v_ref, cap_ref, img_ref, w_ref,
    gq_ref, gk_ref, gv_ref, gp_ref,
    kbuf, vbuf, qbuf, dbuf, cbuf, wsend, abuf, wbuf,
    bias, pbuf, plbuf, dsbuf, atbuf, dobuf,
    esend, erecv, gacc, dsend, drecv, csend, crecv, asend, gslot,
    dkown, dvown, dksend, dvsend, zrk, zrv, dqb, dkb, dvb,
    ssem, rsem, lsem,
):
    dp, seq = lax.axis_index("dp"), lax.axis_index("seq")
    c, x = dp % 2, dp // 8
    y, zl = seq % 4, seq // 4
    z = ((dp // 2) % 4) * 2 + zl
    length = len_ref[0]
    here = lambda yy: device(x, yy, z, c)
    mate_z = device(x, y, z + 1 - 2 * zl, c)
    mate_c = device(x, y, z, 1 - c)
    on_diagonal = x == y
    count = [0]
    pending = []

    def slots(n):
        count[0] += n
        return count[0] - n

    def send(src, dst, to, ssl, rsl=None):
        cp = pltpu.make_async_remote_copy(
            src_ref=src, dst_ref=dst, send_sem=ssem.at[ssl], recv_sem=rsem.at[ssl if rsl is None else rsl],
            device_id=to, device_id_type=MESH,
        )
        cp.start()
        pending.append(cp)
        return cp

    def cols(index, width):
        return pl.ds(pl.multiple_of(index * width, 128), width)

    nlocal = [0]

    def local(src, dst):
        cp = pltpu.make_async_copy(src, dst, lsem.at[nlocal[0]])
        nlocal[0] += 1
        cp.start()
        return cp

    own_k = local(k_ref.at[:, cols(y, 384)], kbuf.at[0, y])
    own_v = local(v_ref.at[:, cols(y, 384)], vbuf.at[0, y])
    own_q = local(q_ref.at[:, cols(y, 384)], qbuf.at[y])
    own_d = local(img_ref, dbuf.at[y, pl.ds(16, 112)])
    own_c = local(cap_ref.at[:, cols(y, 384)], cbuf.at[y])

    w = w_ref[...].astype(F32)
    w = jnp.concatenate([w, jnp.zeros((10, 1536), F32)], axis=0).astype(BF)
    for j in range(4):
        wsend[j] = w[:, j * 384:(j + 1) * 384]
    dbuf[:, 0:16, :] = jnp.zeros((4, 16, 1536), BF)

    barrier = pltpu.get_barrier_semaphore()

    def greet(to):
        pl.semaphore_signal(barrier, inc=1, device_id=to, device_id_type=MESH)

    for i in range(1, 4):
        greet(here((y + i) % 4))
        greet(device((x + i) % 4, y, z, c))
    for i in range(1, 8):
        greet(device(x, y, (z + i) % 8, c))
    greet(mate_c)
    for j in range(4):
        @pl.when(jnp.logical_not(on_diagonal & (x == j)))
        def _():
            greet(device(j, x, z, c))

        @pl.when(jnp.logical_not(on_diagonal & (y == j)))
        def _():
            greet(device(y, j, z, c))
    pl.semaphore_wait(barrier, 22 - 2 * on_diagonal.astype(jnp.int32))

    kv = []
    base = slots(6)
    for i in range(1, 4):
        p = (y + i) % 4
        a = send(k_ref.at[:, cols(p, 384)], kbuf.at[0, y], here(p), base + 2 * i - 2)
        b = send(v_ref.at[:, cols(p, 384)], vbuf.at[0, y], here(p), base + 2 * i - 1)
        kv.append((a, b))
    zbase = slots(8)
    zk = [send(k_ref.at[:, cols(y, 384)], kbuf.at[1, y], mate_z, zbase)]
    zv = [send(v_ref.at[:, cols(y, 384)], vbuf.at[1, y], mate_z, zbase + 1)]

    wa = slots(4)

    def wa_copy(j, to):
        return pltpu.make_async_remote_copy(
            src_ref=wsend.at[j], dst_ref=abuf.at[y], send_sem=ssem.at[wa + j], recv_sem=rsem.at[wa + y],
            device_id=to, device_id_type=MESH,
        )

    def wa_local(j):
        return pltpu.make_async_copy(wsend.at[j], abuf.at[y], lsem.at[7])

    for j in range(4):
        mine = on_diagonal & (x == j)

        @pl.when(mine)
        def _():
            wa_local(j).start()

        @pl.when(jnp.logical_not(mine))
        def _():
            wa_copy(j, device(j, x, z, c)).start()
    for j in range(4):
        mine = on_diagonal & (x == j)

        @pl.when(mine)
        def _():
            wa_local(j).wait()

        @pl.when(jnp.logical_not(mine))
        def _():
            wa_copy(j, device(j, x, z, c)).wait_send()
            pltpu.make_async_remote_copy(
                src_ref=wsend.at[j], dst_ref=abuf.at[j], send_sem=ssem.at[wa + j], recv_sem=rsem.at[wa + j],
                device_id=mate_c, device_id_type=MESH,
            ).wait_recv()
    rows = jnp.concatenate([abuf[j].astype(F32)[0:8] for j in range(4)], axis=0).astype(BF)
    zrows = lambda zz: pl.ds(pl.multiple_of(zz * 32, 32), 32)
    wbuf[c, x, zrows(z), :] = rows
    wc = []
    base = slots(7)
    for i in range(1, 8):
        piece = wbuf.at[c, x, zrows(z)]
        wc.append(send(piece, piece, device(x, y, (z + i) % 8, c), base + i - 1))

    own_k.wait()
    own_v.wait()
    for i in (1, 3, 2):
        p = (y + 4 - i) % 4
        a, b = kv[i - 1]
        a.wait_recv()
        zk.append(send(kbuf.at[0, p], kbuf.at[1, p], mate_z, zbase + 2 * i))
        b.wait_recv()
        zv.append(send(vbuf.at[0, p], vbuf.at[1, p], mate_z, zbase + 2 * i + 1))
    base = slots(9)
    qs, ds, cs = [], [], []
    for i in range(1, 4):
        p = (y + i) % 4
        qs.append(send(q_ref.at[:, cols(p, 384)], qbuf.at[y], here(p), base + i - 1))
    for i in range(1, 4):
        p = (y + i) % 4
        cs.append(send(cap_ref.at[:, cols(p, 384)], cbuf.at[y], here(p), base + 2 + i))
        ds.append(send(img_ref, dbuf.at[y, pl.ds(16, 112)], here(p), base + 5 + i))

    for cp in wc:
        cp.wait_recv()
    wd = []
    base = slots(3)
    for i in range(1, 4):
        wd.append(send(wbuf.at[c, x], wbuf.at[c, x], device((x + i) % 4, y, z, c), base + i - 1))

    ki = lax.broadcasted_iota(jnp.int32, (1024, 256), 0)
    blk = jnp.where(ki < 512, zl, 1 - zl) * 4 + (ki // 128) % 4
    off = ki % 128
    token = blk * 112 + off - 16
    bias[...] = jnp.where((off < 16) | (token < length), 0.0, NEG)

    own_q.wait()
    for cp in qs + zk + zv:
        cp.wait_recv()

    def forward(h):
        lanes = slice(h * 128, (h + 1) * 128)
        kk = kbuf[:, :, :, lanes].reshape(1024, 128)
        vv = vbuf[:, :, :, lanes].reshape(1024, 128)
        for t in range(2):
            qq = qbuf[2 * t:2 * t + 2, :, lanes].reshape(256, 128)
            s = dot(kk, qq, NT) + bias[...]
            top = jnp.max(s, axis=0, keepdims=True)
            e = jnp.exp2((s - top) * (SCALE * LOG2E))
            prob = e * (1.0 / jnp.sum(e, axis=0, keepdims=True))
            low = prob.astype(BF)
            pbuf[h, :, t * 256:(t + 1) * 256] = prob
            plbuf[h, :, t * 256:(t + 1) * 256] = low
            atbuf[h * 128:(h + 1) * 128, t * 256:(t + 1) * 256] = dot(vv, low, TT).astype(BF)

    forward(0)
    for cp in wd:
        cp.wait_recv()
    we = send(wbuf.at[c], wbuf.at[c], mate_c, slots(1))
    forward(1)
    forward(2)

    own_d.wait()
    own_c.wait()
    for cp in ds + cs:
        cp.wait_recv()
    qi = lax.broadcasted_iota(jnp.int32, (384, 512), 1)
    off = qi % 128
    token = (zl * 4 + qi // 128) * 112 + off - 16
    image = (off >= 16) & (token < length)
    at_image = jnp.where(image, atbuf[...].astype(F32), 0.0).astype(BF)

    def project(half):
        padded = dot(select_rows(half), at_image, NN).astype(BF)
        return [dot(padded, dbuf[:, :, j * 384:(j + 1) * 384].reshape(512, 384), NN) for j in range(4)]

    for j, part in enumerate(project(1 - c)):
        esend[j] = part.astype(BF)
    ge = send(esend, erecv, mate_c, slots(1))
    for j, part in enumerate(project(c)):
        gacc[j] = part

    we.wait_recv()
    do_all = jnp.zeros((512, 384), F32)
    for half in range(2):
        padded = jnp.zeros((512, 256), F32)
        for j in range(4):
            padded += dot(dbuf[:, :, j * 384:(j + 1) * 384].reshape(512, 384), wbuf[half, j], NT)
        do_all += dot(padded.astype(BF), select_rows(half), NN)
    ri = lax.broadcasted_iota(jnp.int32, (512, 384), 0)
    token = (zl * 4 + ri // 128) * 112 + ri % 128 - 16
    dobuf[...] = jnp.where(token < length, do_all, 0.0).astype(BF)
    for p in range(4):
        dobuf[p * 128:p * 128 + 16, :] = cbuf[p]

    ge.wait_recv()
    for j in range(4):
        total = gacc[j] + erecv[j].astype(F32)
        gacc[j] = total
        dsend[j] = total.astype(BF)
    base = slots(3)
    gd = []
    for i in range(1, 4):
        xx = (x + i) % 4
        gd.append(send(dsend.at[xx], drecv.at[i - 1], device(xx, y, z, c), base + i - 1))

    ybase = slots(27)
    zrbase = slots(6)
    zsent = []

    def to_rows(src, out, which, h):
        cps = []
        lane = cols(y * 3 + h, 128)
        for i in range(1, 4):
            p = (y + i) % 4
            piece = src.at[h, pl.ds(pl.multiple_of(p * 128, 128), 128)]
            cps.append(send(piece, out.at[:, lane], here(p), ybase + which * 9 + h * 3 + i - 1))
        piece = src.at[h, pl.ds(pl.multiple_of(y * 128, 128), 128)]
        return cps, local(piece, out.at[:, lane])

    nlocal[0] = 8
    results = []

    def backward(h):
        lanes = slice(h * 128, (h + 1) * 128)
        kk = kbuf[:, :, :, lanes].reshape(1024, 128)
        vv = vbuf[:, :, :, lanes].reshape(1024, 128)
        for t in range(2):
            part = slice(t * 256, (t + 1) * 256)
            do = dobuf[part, lanes]
            delta = jnp.sum(do.astype(F32).T * atbuf[lanes, part].astype(F32), axis=0, keepdims=True)
            dsbuf[:, part] = (pbuf[h, :, part] * (dot(vv, do, NT) - delta)).astype(BF)
        dv = dot(plbuf[h], dobuf[:, lanes], NN)
        dvown[h] = dv[0:512]
        dvsend[h] = dv[512:1024].astype(BF)
        dk = dot(dsbuf[...], qbuf[:, :, lanes].reshape(512, 128), NN) * SCALE
        dkown[h] = dk[0:512]
        dksend[h] = dk[512:1024].astype(BF)
        zsent.append((
            send(dksend.at[h], zrk.at[h], mate_z, zrbase + 2 * h),
            send(dvsend.at[h], zrv.at[h], mate_z, zrbase + 2 * h + 1),
        ))
        dqb[h] = (dot(kk, dsbuf[...], TT) * SCALE).T.astype(BF)
        results.append(to_rows(dqb, gq_ref, 0, h))

    def settle(h):
        a, b = zsent[h]
        a.wait_recv()
        dkb[h] = (dkown[h] + zrk[h].astype(F32)).astype(BF)
        results.append(to_rows(dkb, gk_ref, 1, h))
        b.wait_recv()
        dvb[h] = (dvown[h] + zrv[h].astype(F32)).astype(BF)
        results.append(to_rows(dvb, gv_ref, 2, h))

    backward(0)
    for cp in gd:
        cp.wait_recv()
    total = gacc[x] + drecv[0].astype(F32) + drecv[1].astype(F32) + drecv[2].astype(F32)
    gacc[x] = total
    csend[...] = total.astype(BF).reshape(8, 32, 384)
    base = slots(7)
    gc = []
    for i in range(1, 8):
        zz = (z + i) % 8
        gc.append(send(csend.at[zz], crecv.at[i - 1], device(x, y, zz, c), base + i - 1))

    backward(1)
    for cp in gc:
        cp.wait_recv()
    total = gacc[x, zrows(z), :]
    for i in range(7):
        total += crecv[i].astype(F32)
    asend[...] = total
    ga = slots(4)

    def ga_copy(j, to):
        return pltpu.make_async_remote_copy(
            src_ref=asend.at[pl.ds(j * 8, 8)], dst_ref=gslot.at[x], send_sem=ssem.at[ga + j], recv_sem=rsem.at[ga + x],
            device_id=to, device_id_type=MESH,
        )

    def ga_local(j):
        return pltpu.make_async_copy(asend.at[pl.ds(j * 8, 8)], gslot.at[x], lsem.at[6])

    for j in range(4):
        mine = on_diagonal & (y == j)

        @pl.when(mine)
        def _():
            ga_local(j).start()

        @pl.when(jnp.logical_not(mine))
        def _():
            ga_copy(j, device(y, j, z, c)).start()

    backward(2)
    for h in range(3):
        settle(h)
    for j in range(4):
        mine = on_diagonal & (y == j)

        @pl.when(mine)
        def _():
            ga_local(j).wait()

        @pl.when(jnp.logical_not(mine))
        def _():
            ga_copy(j, device(y, j, z, c)).wait_send()
            pltpu.make_async_remote_copy(
                src_ref=asend.at[pl.ds(j * 8, 8)], dst_ref=gslot.at[j], send_sem=ssem.at[ga + j],
                recv_sem=rsem.at[ga + j], device_id=mate_c, device_id_type=MESH,
            ).wait_recv()
    for j in range(4):
        gp_ref[:, j * 384:(j + 1) * 384] = gslot[j][0:6]
    for cps, own in results:
        for cp in cps:
            cp.wait_recv()
        own.wait()
    for cp in pending:
        cp.wait_send()
    assert count[0] <= 100 and nlocal[0] <= 20


def shards(query_rows, key_rows, value_rows, d_caption, d_image, proj_weight, lengths):
    rows = jax.ShapeDtypeStruct((128, 1536), BF)
    hbm = pl.BlockSpec(memory_space=pl.ANY)
    vmem = pl.BlockSpec(memory_space=pltpu.VMEM)
    scratch = [
        pltpu.VMEM(shape, dtype)
        for shape, dtype in (
            ((2, 4, 128, 384), BF), ((2, 4, 128, 384), BF), ((4, 128, 384), BF), ((4, 128, 1536), BF),
            ((4, 16, 384), BF), ((4, 16, 384), BF), ((4, 16, 384), BF), ((2, 4, 256, 384), BF),
            ((1024, 256), F32), ((3, 1024, 512), F32), ((3, 1024, 512), BF), ((1024, 512), BF),
            ((384, 512), BF), ((512, 384), BF),
            ((4, 256, 384), BF), ((4, 256, 384), BF), ((4, 256, 384), F32), ((4, 256, 384), BF),
            ((3, 256, 384), BF), ((8, 32, 384), BF), ((7, 32, 384), BF), ((32, 384), F32), ((4, 8, 384), F32),
            ((3, 512, 128), F32), ((3, 512, 128), F32), ((3, 512, 128), BF), ((3, 512, 128), BF),
            ((3, 512, 128), BF), ((3, 512, 128), BF), ((3, 512, 128), BF), ((3, 512, 128), BF), ((3, 512, 128), BF),
        )
    ]
    return pl.pallas_call(
        kernel,
        out_shape=(rows, rows, rows, jax.ShapeDtypeStruct((6, 1536), F32)),
        in_specs=[pl.BlockSpec(memory_space=pltpu.SMEM), hbm, hbm, hbm, hbm, hbm, vmem],
        out_specs=(hbm, hbm, hbm, vmem),
        scratch_shapes=scratch + [
            pltpu.SemaphoreType.DMA((100,)), pltpu.SemaphoreType.DMA((100,)), pltpu.SemaphoreType.DMA((20,)),
        ],
        compiler_params=pltpu.CompilerParams(
            collective_id=0, has_side_effects=True, vmem_limit_bytes=56 * 2**20
        ),
        name="joint_attention_backward",
    )(lengths, query_rows, key_rows, value_rows, d_caption, d_image, proj_weight)


def solution(mesh):
    placed = P(("dp", "seq"), None)
    return jax.shard_map(
        shards,
        mesh=mesh,
        in_specs=(placed,) * 6 + (P("dp"),),
        out_specs=(placed,) * 4,
        check_vma=False,
    )
```

time: 2260 us -> 89.3 us (0.04)
  the two profiles are of different devices: /device:TPU:4 before, /device:TPU:1 now
where the time goes in v1:
time: 89.3 us; the launch traced here: 89 us
  Pallas kernels  83.4 us (93%)
  local copies, waits for them, and re-layouts  4.37 us (5%)
  between operations  1.3 us (1%)
    pallas_call x1, Pallas kernels, shards(): pl.pallas_call(kernel, out_shape=(rows, rows, rows, jax.ShapeDtypeStruct(...  83.4 us
    unnamed x10, local copies, waits for them, and re-layouts  4.37 us

profile of v1, /device:TPU:1, one launch (start us, length us, event | category | flops | bytes accessed | tf_op | source)
XLA Modules:
  0.0 89.0 jit_solution(2119041902832504045)
XLA Ops:
  1.3 83.4 %joint_attention_backward.1 = (bf16[128,1536]{1,0:T(8,128)(2,1)}, bf16[128,1536]{1,0:T(8,128)(2,1)}, bf16[128,1536]{1,0:T(8,128)(2,1)}, f32[6,1536]{1,0:T(8,128)}) custom-call(s32[1]{0:T(128)S(6)} %copy.15.len_ref, bf16[128,1536]{1,0:T(8,128)(2,1)} %q_ref.1, bf16[128,1536]{1,0:T(8,128)(2,1)} %k_ref.1, bf16[128,1536]{1,0:T(8,128)(2,1)} %v_ref.1, ...), custom_call_target="tpu_custom_call" | custom-call | tf_op jit(solution)/shard_map/joint_attention_backward/pallas_call | solution.py:404
  84.7 0.0 copy-start.1
  84.7 1.8 %copy.16 = bf16[128,1536]{1,0:T(8,128)(2,1)} copy(bf16[128,1536]{1,0:T(8,128)(2,1)} %get-tuple-element.8) | data formatting | bytes 786432
  86.5 0.0 copy-done.1
  86.5 0.0 copy-start
  86.5 0.7 copy.17
  87.2 0.4 copy-done
  87.6 0.0 copy-start.2
  87.6 0.7 copy.18
  88.4 0.1 copy-done.2
  88.4 0.6 copy.19
Async XLA Ops:
  84.7 1.8 %copy-start.1 = (bf16[128,1536]{1,0:T(8,128)(2,1)S(1)}, bf16[128,1536]{1,0:T(8,128)(2,1)}, u32[]{:S(2)}) copy-start(bf16[128,1536]{1,0:T(8,128)(2,1)} %get-tuple-element.9) | copy-start | bytes 1179652
  86.5 1.1 %copy-start = (bf16[128,1536]{1,0:T(8,128)(2,1)S(1)}, bf16[128,1536]{1,0:T(8,128)(2,1)}, u32[]{:S(2)}) copy-start(bf16[128,1536]{1,0:T(8,128)(2,1)} %get-tuple-element.10) | copy-start | bytes 1179652
  87.6 0.8 copy-start.2

commit v2 on v1

v2 whole, which is shorter than its diff:
```python
import jax
import jax.numpy as jnp
from jax import lax
from jax.experimental import pallas as pl
from jax.experimental.pallas import tpu as pltpu
from jax.sharding import PartitionSpec as P

MESH = pl.DeviceIdType.MESH
F32, BF = jnp.float32, jnp.bfloat16
SCALE = 128 ** (-0.5)
EXP_SCALE = SCALE * 1.4426950408889634
NEG = -1e30
NT = (((1,), (1,)), ((), ()))
TT = (((0,), (0,)), ((), ()))
NN = (((1,), (0,)), ((), ()))
SEMS, LOCALS = 180, 32


def dot(a, b, dims):
    return lax.dot_general(a, b, dims, preferred_element_type=F32)


def device(x, y, z, c):
    return ((x * 4 + z // 2) * 2 + c, (z % 2) * 4 + y)


def select(rows, cols, pick):
    r = lax.broadcasted_iota(jnp.int32, (rows, cols), 0)
    c = lax.broadcasted_iota(jnp.int32, (rows, cols), 1)
    return jnp.where(pick(r, c), 1.0, 0.0).astype(BF)


def kernel(
    len_ref, q_ref, k_ref, v_ref, cap_ref, img_ref, w_ref,
    gq_ref, gk_ref, gv_ref, gp_ref,
    kvb, qb, dbuf, cbuf, wsend, abuf, wz, wbuf,
    bias, pbuf, lowbuf, dsbuf, p2buf, low2buf, ds2buf, atbuf, dob, lse, delta,
    esend, erecv, gacc, dsend, drecv, csend, crecv, asend, gslot,
    dkown, dvown, dqb, dkb, dvb,
    ssem, rsem, lsem,
):
    dp, seq = lax.axis_index("dp"), lax.axis_index("seq")
    c, x = dp % 2, dp // 8
    y, zl = seq % 4, seq // 4
    z = ((dp // 2) % 4) * 2 + zl
    length = len_ref[0]
    mate_z = device(x, y, z + 1 - 2 * zl, c)
    mate_c = device(x, y, z, 1 - c)
    on_diagonal = x == y
    count = [0, 0]
    pending = []

    def at_y(yy):
        return device(x, yy, z, c)

    def slots(n):
        count[0] += n
        return count[0] - n

    def send(src, dst, to, slot):
        cp = pltpu.make_async_remote_copy(
            src_ref=src, dst_ref=dst, send_sem=ssem.at[slot], recv_sem=rsem.at[slot],
            device_id=to, device_id_type=MESH,
        )
        cp.start()
        pending.append(cp)
        return cp

    def local(src, dst):
        cp = pltpu.make_async_copy(src, dst, lsem.at[count[1]])
        count[1] += 1
        cp.start()
        return cp

    def cols(index, width):
        return pl.ds(pl.multiple_of(index * width, 128), width)

    def rows(index, height):
        return pl.ds(pl.multiple_of(index * height, height), height)

    barrier = pltpu.get_barrier_semaphore()

    def greet(to):
        pl.semaphore_signal(barrier, inc=1, device_id=to, device_id_type=MESH)

    for i in range(1, 4):
        greet(at_y((y + i) % 4))
        greet(device((x + i) % 4, y, z, c))
    for i in range(1, 8):
        greet(device(x, y, (z + i) % 8, c))
    greet(mate_c)
    for j in range(4):
        @pl.when(jnp.logical_not(on_diagonal & (x == j)))
        def _():
            greet(device(j, x, z, c))

        @pl.when(jnp.logical_not(on_diagonal & (y == j)))
        def _():
            greet(device(y, j, z, c))
    own = []
    for h in range(3):
        lane = cols(y * 3 + h, 128)
        own.append(local(k_ref.at[:, lane], kvb.at[h, 0, y, 0]))
        own.append(local(v_ref.at[:, lane], kvb.at[h, 0, y, 1]))
        own.append(local(q_ref.at[:, lane], qb.at[h, 0, y]))
    own.append(local(img_ref, dbuf.at[y, pl.ds(16, 112)]))
    own.append(local(cap_ref.at[:, cols(y, 384)], cbuf.at[y]))

    w = jnp.concatenate([w_ref[...].astype(F32), jnp.zeros((10, 1536), F32)], axis=0).astype(BF)
    for j in range(4):
        wsend[j] = w[:, j * 384:(j + 1) * 384]
    dbuf[:, 0:16, :] = jnp.zeros((4, 16, 1536), BF)

    ki = lax.broadcasted_iota(jnp.int32, (1024, 256), 0)
    blk = jnp.where(ki < 512, zl, 1 - zl) * 4 + (ki // 128) % 4
    off = ki % 128
    bias[...] = jnp.where((off < 16) | (blk * 112 + off - 16 < length), 0.0, NEG)
    for cp in own:
        cp.wait()

    pl.semaphore_wait(barrier, 22 - 2 * on_diagonal.astype(jnp.int32))

    wa = slots(4)

    def wa_copy(j, to):
        return pltpu.make_async_remote_copy(
            src_ref=wsend.at[j], dst_ref=abuf.at[y], send_sem=ssem.at[wa + j], recv_sem=rsem.at[wa + y],
            device_id=to, device_id_type=MESH,
        )

    def wa_local(j):
        return pltpu.make_async_copy(wsend.at[j], abuf.at[y], lsem.at[LOCALS - 1])

    for j in range(4):
        mine = on_diagonal & (x == j)

        @pl.when(mine)
        def _():
            wa_local(j).start()

        @pl.when(jnp.logical_not(mine))
        def _():
            wa_copy(j, device(j, x, z, c)).start()

    ybase = slots(27)
    came = [[] for _ in range(3)]

    def exchange(h):
        for i in (1, 3, 2):
            p = (y + i) % 4
            lane = cols(p * 3 + h, 128)
            slot = ybase + 9 * h + 3 * (i - 1)
            came[h].append((
                (y + 4 - i) % 4, i,
                send(k_ref.at[:, lane], kvb.at[h, 0, y, 0], at_y(p), slot),
                send(v_ref.at[:, lane], kvb.at[h, 0, y, 1], at_y(p), slot + 1),
                send(q_ref.at[:, lane], qb.at[h, 0, y], at_y(p), slot + 2),
            ))

    zbase = slots(24)
    far_kv, far_q = [[] for _ in range(3)], [[] for _ in range(3)]

    def pass_kv(h, p, i):
        far_kv[h].append(send(kvb.at[h, 0, p], kvb.at[h, 1, p], mate_z, zbase + 4 * h + i))

    def pass_q(h, p, i):
        far_q[h].append(send(qb.at[h, 0, p], qb.at[h, 1, p], mate_z, zbase + 12 + 4 * h + i))

    exchange(0)
    for h in range(3):
        pass_kv(h, y, 0)
    exchange(1)
    exchange(2)

    dbase = slots(4)
    mine_d = dbuf.at[y, pl.ds(16, 112)]
    ds = [send(mine_d, mine_d, at_y((y + 1) % 4), dbase), send(mine_d, mine_d, at_y((y + 3) % 4), dbase + 1)]
    capbase = slots(3)
    cs = [
        send(cap_ref.at[:, cols((y + i) % 4, 384)], cbuf.at[y], at_y((y + i) % 4), capbase + i - 1)
        for i in range(1, 4)
    ]
    for j in range(4):
        mine = on_diagonal & (x == j)

        @pl.when(mine)
        def _():
            wa_local(j).wait()

        @pl.when(jnp.logical_not(mine))
        def _():
            wa_copy(j, device(j, x, z, c)).wait_send()
            pltpu.make_async_remote_copy(
                src_ref=wsend.at[j], dst_ref=abuf.at[j], send_sem=ssem.at[wa + j], recv_sem=rsem.at[wa + j],
                device_id=mate_c, device_id_type=MESH,
            ).wait_recv()
    padded = jnp.concatenate([abuf[j].astype(F32)[0:8] for j in range(4)], axis=0).astype(BF)
    squeeze = select(32, 32, lambda r, k: (k % 8 < 6) & (r == k // 8 * 6 + k % 8))
    wz[z] = dot(squeeze, padded, NN).astype(BF)
    base = slots(7)
    wc = [send(wz.at[z], wz.at[z], device(x, y, (z + i) % 8, c), base + i - 1) for i in range(1, 8)]

    def pass_on(h):
        for p, i, a, b, _ in came[h]:
            a.wait_recv()
            b.wait_recv()
            pass_kv(h, p, i)

    pass_on(0)
    pass_on(1)
    for cp in wc:
        cp.wait_recv()
    wbuf[c, x] = jnp.concatenate([wz[i].astype(F32)[0:24] for i in range(8)], axis=0).astype(BF)
    base = slots(4)
    wd = [
        send(wbuf.at[c, x], wbuf.at[c, x], device((x + 1) % 4, y, z, c), base),
        send(wbuf.at[c, x], wbuf.at[c, x], device((x + 3) % 4, y, z, c), base + 1),
    ]
    pass_on(2)
    for h in range(3):
        pass_q(h, y, 0)
        for p, i, _, _, q in came[h]:
            q.wait_recv()
            pass_q(h, p, i)

    def whole(buf, h, which):
        return buf[h, :, :, which].reshape(1024, 128)

    def forward(h):
        for cp in far_kv[h]:
            cp.wait_recv()
        kk, vv = whole(kvb, h, 0), whole(kvb, h, 1)
        for t in range(2):
            part = slice(t * 256, (t + 1) * 256)
            qq = qb[h, 0, 2 * t:2 * t + 2].reshape(256, 128)
            s = dot(kk, qq, NT) + bias[...]
            top = jnp.max(s, axis=0, keepdims=True)
            e = jnp.exp2((s - top) * EXP_SCALE)
            total = jnp.sum(e, axis=0, keepdims=True)
            prob = e * (1.0 / total)
            low = prob.astype(BF)
            pbuf[h, :, part] = prob
            lowbuf[h, :, part] = low
            atbuf[h * 128:(h + 1) * 128, part] = dot(vv, low, TT).astype(BF)
            lse[0, h:h + 1, part] = top * EXP_SCALE + jnp.log2(total)

    forward(0)
    for cp in wd:
        cp.wait_recv()
    low_half = wbuf.at[c, (x + 3) % 4, pl.ds(0, 96)]
    high_half = wbuf.at[c, (x + 1) % 4, pl.ds(96, 96)]
    wd2 = [
        send(low_half, low_half, device((x + 1) % 4, y, z, c), base + 2),
        send(high_half, high_half, device((x + 3) % 4, y, z, c), base + 3),
    ]
    forward(1)
    ds[0].wait_recv()
    piece = dbuf.at[(y + 3) % 4, pl.ds(16, 64)]
    ds.append(send(piece, piece, at_y((y + 1) % 4), dbase + 2))
    ds[1].wait_recv()
    piece = dbuf.at[(y + 1) % 4, pl.ds(80, 48)]
    ds.append(send(piece, piece, at_y((y + 3) % 4), dbase + 3))

    for cp in wd2:
        cp.wait_recv()
    we = send(wbuf.at[c], wbuf.at[c], mate_c, slots(1))
    forward(2)
    stat = slots(2)
    far_lse = send(lse.at[0], lse.at[1], mate_z, stat)

    qi = lax.broadcasted_iota(jnp.int32, (384, 512), 1)
    off = qi % 128
    token = (zl * 4 + qi // 128) * 112 + off - 16
    at_image = jnp.where((off >= 16) & (token < length), atbuf[...].astype(F32), 0.0)
    blocks = [at_image[i * 48:(i + 1) * 48] for i in range(8)]
    ones = jnp.zeros((48, 512), jnp.int32) + c
    first = jnp.concatenate([jnp.where(ones == 0, blocks[2 * i + 1], blocks[2 * i]) for i in range(4)], axis=0).astype(BF)
    second = jnp.concatenate([jnp.where(ones == 0, blocks[2 * i], blocks[2 * i + 1]) for i in range(4)], axis=0).astype(BF)
    for cp in cs:
        cp.wait_recv()
    for cp in ds[2:]:
        cp.wait_recv()

    def image_cols(j):
        return dbuf[:, :, j * 384:(j + 1) * 384].reshape(512, 384)

    for j in range(4):
        esend[j] = dot(first, image_cols(j), NN).astype(BF)
    ge = send(esend, erecv, mate_c, slots(1))

    for j in range(4):
        gacc[j] = dot(second, image_cols(j), NN)

    we.wait_recv()
    do_all = jnp.zeros((512, 384), F32)
    for j in range(4):
        wj = jnp.concatenate(
            [wbuf[i % 2, j, i // 2 * 48:(i // 2 + 1) * 48] for i in range(8)], axis=0
        )
        do_all += dot(image_cols(j), wj, NT)
    ri = lax.broadcasted_iota(jnp.int32, (512, 384), 0)
    token = (zl * 4 + ri // 128) * 112 + ri % 128 - 16
    do_all = jnp.where(token < length, do_all, 0.0).astype(BF)
    dobase = slots(3)
    far_do = []
    for h in range(3):
        lanes = slice(h * 128, (h + 1) * 128)
        for p in range(4):
            dob[h, 0, p, 0:16] = cbuf[p, :, lanes]
            dob[h, 0, p, 16:128] = do_all[p * 128 + 16:(p + 1) * 128, lanes]
        far_do.append(send(dob.at[h, 0], dob.at[h, 1], mate_z, dobase + h))
        for t in range(2):
            part = slice(t * 256, (t + 1) * 256)
            do = dob[h, 0, 2 * t:2 * t + 2].reshape(256, 128)
            delta[0, h:h + 1, part] = jnp.sum(
                do.astype(F32).T * atbuf[lanes, part].astype(F32), axis=0, keepdims=True
            )
    far_delta = send(delta.at[0], delta.at[1], mate_z, stat + 1)

    rbase = slots(27)
    results = []

    def to_rows(src, out, which, h):
        lane = cols(y * 3 + h, 128)
        for i in (1, 3, 2):
            p = (y + i) % 4
            results.append(send(src.at[h, rows(p, 128)], out.at[:, lane], at_y(p), rbase + which * 9 + h * 3 + i - 1))
        finals.append(local(src.at[h, rows(y, 128)], out.at[:, lane]))

    finals = []

    def backward(h):
        kk, vv = whole(kvb, h, 0), whole(kvb, h, 1)
        for t in range(2):
            part = slice(t * 256, (t + 1) * 256)
            do = dob[h, 0, 2 * t:2 * t + 2].reshape(256, 128)
            dsbuf[:, part] = (pbuf[h, :, part] * (dot(vv, do, NT) - delta[0, h:h + 1, part])).astype(BF)
        dqb[h] = (dot(kk, dsbuf[...], TT) * SCALE).T.astype(BF)
        to_rows(dqb, gq_ref, 0, h)
        dvown[h] = dot(lowbuf[h, 0:512], dob[h, 0].reshape(512, 128), NN)
        dkown[h] = dot(dsbuf[0:512], qb[h, 0].reshape(512, 128), NN)

    def far_probs(h):
        for cp in far_q[h]:
            cp.wait_recv()
        kk = kvb[h, 0, :, 0].reshape(512, 128)
        for t in range(2):
            part = slice(t * 256, (t + 1) * 256)
            s = dot(kk, qb[h, 1, 2 * t:2 * t + 2].reshape(256, 128), NT) + bias[0:512]
            prob = jnp.exp2(s * EXP_SCALE - lse[1, h:h + 1, part])
            p2buf[h, :, part] = prob
            low2buf[h, :, part] = prob.astype(BF)

    def far_backward(h):
        far_do[h].wait_recv()
        vv = kvb[h, 0, :, 1].reshape(512, 128)
        for t in range(2):
            part = slice(t * 256, (t + 1) * 256)
            do = dob[h, 1, 2 * t:2 * t + 2].reshape(256, 128)
            ds2buf[:, part] = (p2buf[h, :, part] * (dot(vv, do, NT) - delta[1, h:h + 1, part])).astype(BF)
        dkb[h] = ((dkown[h] + dot(ds2buf[...], qb[h, 1].reshape(512, 128), NN)) * SCALE).astype(BF)
        to_rows(dkb, gk_ref, 1, h)
        dvb[h] = (dvown[h] + dot(low2buf[h], dob[h, 1].reshape(512, 128), NN)).astype(BF)
        to_rows(dvb, gv_ref, 2, h)

    ge.wait_recv()
    for j in range(4):
        total = gacc[j] + erecv[j].astype(F32)
        gacc[j] = total
        dsend[j] = total.astype(BF)
    base = slots(3)
    gd = []
    for i in range(1, 4):
        xx = (x + i) % 4
        gd.append(send(dsend.at[xx], drecv.at[i - 1], device(xx, y, z, c), base + i - 1))
    backward(0)
    backward(1)
    backward(2)
    far_lse.wait_recv()
    for h in range(3):
        far_probs(h)
    far_delta.wait_recv()
    far_backward(0)
    far_backward(1)

    for cp in gd:
        cp.wait_recv()
    total = gacc[x] + drecv[0].astype(F32) + drecv[1].astype(F32) + drecv[2].astype(F32)
    spread = select(256, 192, lambda r, k: (r % 8 < 6) & (k == r // 8 * 6 + r % 8))
    csend[...] = dot(spread, total.astype(BF), NN).astype(BF).reshape(8, 32, 384)
    base = slots(7)
    gc = []
    for i in range(1, 8):
        zz = (z + i) % 8
        gc.append(send(csend.at[zz], crecv.at[i - 1], device(x, y, zz, c), base + i - 1))
    far_backward(2)

    total = csend[z].astype(F32)
    for i in range(7):
        gc[i].wait_recv()
        total += crecv[i].astype(F32)
    asend[...] = total
    ga = slots(4)

    def ga_copy(j, to):
        return pltpu.make_async_remote_copy(
            src_ref=asend.at[pl.ds(j * 8, 8)], dst_ref=gslot.at[x], send_sem=ssem.at[ga + j], recv_sem=rsem.at[ga + x],
            device_id=to, device_id_type=MESH,
        )

    def ga_local(j):
        return pltpu.make_async_copy(asend.at[pl.ds(j * 8, 8)], gslot.at[x], lsem.at[LOCALS - 2])

    for j in range(4):
        mine = on_diagonal & (y == j)

        @pl.when(mine)
        def _():
            ga_local(j).start()

        @pl.when(jnp.logical_not(mine))
        def _():
            ga_copy(j, device(y, j, z, c)).start()

    for j in range(4):
        mine = on_diagonal & (y == j)

        @pl.when(mine)
        def _():
            ga_local(j).wait()

        @pl.when(jnp.logical_not(mine))
        def _():
            ga_copy(j, device(y, j, z, c)).wait_send()
            pltpu.make_async_remote_copy(
                src_ref=asend.at[pl.ds(j * 8, 8)], dst_ref=gslot.at[j], send_sem=ssem.at[ga + j],
                recv_sem=rsem.at[ga + j], device_id=mate_c, device_id_type=MESH,
            ).wait_recv()
    for j in range(4):
        gp_ref[:, j * 384:(j + 1) * 384] = gslot[j][0:6]
    for cp in results:
        cp.wait_recv()
    for cp in finals:
        cp.wait()
    for cp in pending:
        cp.wait_send()
    assert count[0] <= SEMS and count[1] <= LOCALS - 2


def copy_out(*refs):
    half = len(refs) // 2
    for src, dst in zip(refs[:half], refs[half:]):
        dst[...] = src[...]


def shards(query_rows, key_rows, value_rows, d_caption, d_image, proj_weight, lengths):
    block = jax.ShapeDtypeStruct((128, 1536), BF)
    outs = (block, block, block, jax.ShapeDtypeStruct((6, 1536), F32))
    hbm = pl.BlockSpec(memory_space=pl.ANY)
    vmem = pl.BlockSpec(memory_space=pltpu.VMEM)
    scratch = [
        pltpu.VMEM(shape, dtype)
        for shape, dtype in (
            ((3, 2, 4, 2, 128, 128), BF), ((3, 2, 4, 128, 128), BF), ((4, 128, 1536), BF), ((4, 16, 384), BF),
            ((4, 16, 384), BF), ((4, 16, 384), BF), ((8, 32, 384), BF), ((2, 4, 192, 384), BF),
            ((1024, 256), F32), ((3, 1024, 512), F32), ((3, 1024, 512), BF), ((1024, 512), BF),
            ((3, 512, 512), F32), ((3, 512, 512), BF), ((512, 512), BF),
            ((384, 512), BF), ((3, 2, 4, 128, 128), BF), ((2, 8, 512), F32), ((2, 8, 512), F32),
            ((4, 192, 384), BF), ((4, 192, 384), BF), ((4, 192, 384), F32), ((4, 192, 384), BF),
            ((3, 192, 384), BF), ((8, 32, 384), BF), ((7, 32, 384), BF), ((32, 384), F32), ((4, 8, 384), F32),
            ((3, 512, 128), F32), ((3, 512, 128), F32),
            ((3, 512, 128), BF), ((3, 512, 128), BF), ((3, 512, 128), BF),
        )
    ]
    results = pl.pallas_call(
        kernel,
        out_shape=outs,
        in_specs=[pl.BlockSpec(memory_space=pltpu.SMEM), hbm, hbm, hbm, hbm, hbm, vmem],
        out_specs=(hbm, hbm, hbm, vmem),
        scratch_shapes=scratch + [
            pltpu.SemaphoreType.DMA((SEMS,)), pltpu.SemaphoreType.DMA((SEMS,)), pltpu.SemaphoreType.DMA((LOCALS,)),
        ],
        compiler_params=pltpu.CompilerParams(
            collective_id=0, has_side_effects=True, vmem_limit_bytes=56 * 2**20
        ),
        name="joint_attention_backward",
    )(lengths, query_rows, key_rows, value_rows, d_caption, d_image, proj_weight)
    return pl.pallas_call(
        copy_out,
        out_shape=outs,
        in_specs=[vmem] * 4,
        out_specs=(vmem,) * 4,
        name="copy_out",
    )(*results)


def solution(mesh):
    placed = P(("dp", "seq"), None)
    return jax.shard_map(
        shards,
        mesh=mesh,
        in_specs=(placed,) * 6 + (P("dp"),),
        out_specs=(placed,) * 4,
        check_vma=False,
    )
```

time: 89.3 us -> 71 us (0.80)
  the two profiles are of different devices: /device:TPU:1 before, /device:TPU:4 now
where the time goes in v2:
time: 71 us; the launch traced here: 70.5 us
  Pallas kernels  69.3 us (98%)
  between operations  1.29 us (2%)
    pallas_call x1, Pallas kernels, shards(): pl.pallas_call(kernel, out_shape=outs, in_specs=[pl.BlockSpec(memory_spac...  67 us
    pallas_call x1, Pallas kernels, shards(): pl.pallas_call(copy_out, out_shape=outs, in_specs=[vmem] * 4, out_specs=(...  2.27 us

profile of v2, /device:TPU:4, one launch (start us, length us, event | category | flops | bytes accessed | tf_op | source)
XLA Modules:
  0.0 70.5 jit_solution(14267081526098022746)
XLA Ops:
  1.3 67.0 %joint_attention_backward.1 = (bf16[128,1536]{1,0:T(8,128)(2,1)}, bf16[128,1536]{1,0:T(8,128)(2,1)}, bf16[128,1536]{1,0:T(8,128)(2,1)}, f32[6,1536]{1,0:T(8,128)}) custom-call(s32[1]{0:T(128)S(6)} %copy.11.len_ref, bf16[128,1536]{1,0:T(8,128)(2,1)} %q_ref.1, bf16[128,1536]{1,0:T(8,128)(2,1)} %k_ref.1, bf16[128,1536]{1,0:T(8,128)(2,1)} %v_ref.1, ...), custom_call_target="tpu_custom_call" | custom-call | tf_op jit(solution)/shard_map/joint_attention_backward/pallas_call | solution.py:475
  68.3 2.3 %copy_out.1 = (bf16[128,1536]{1,0:T(8,128)(2,1)}, bf16[128,1536]{1,0:T(8,128)(2,1)}, bf16[128,1536]{1,0:T(8,128)(2,1)}, f32[6,1536]{1,0:T(8,128)}) custom-call(bf16[128,1536]{1,0:T(8,128)(2,1)} %get-tuple-element.8.refs_0_, bf16[128,1536]{1,0:T(8,128)(2,1)} %get-tuple-element.9.refs_1_, bf16[128,1536]{1,0:T(8,128)(2,1)} %get-tuple-element.10.refs_2_, ...), custom_call_target="tpu_custom_call" | custom-call | tf_op jit(solution)/shard_map/copy_out/pallas_call | solution.py:488

commit v3 on v2

v3 whole, which is shorter than its diff:
```python
import jax
import jax.numpy as jnp
from jax import lax
from jax.experimental import pallas as pl
from jax.experimental.pallas import tpu as pltpu
from jax.sharding import PartitionSpec as P

MESH = pl.DeviceIdType.MESH
F32, BF = jnp.float32, jnp.bfloat16
SCALE = 128 ** (-0.5)
EXP_SCALE = SCALE * 1.4426950408889634
NEG = -1e30
NT = (((1,), (1,)), ((), ()))
TT = (((0,), (0,)), ((), ()))
NN = (((1,), (0,)), ((), ()))
SEMS, LOCALS = 40, 7


def dot(a, b, dims):
    return lax.dot_general(a, b, dims, preferred_element_type=F32)


def device(x, y, z, c):
    return ((x * 4 + z // 2) * 2 + c, (z % 2) * 4 + y)


def select(rows, cols, pick):
    r = lax.broadcasted_iota(jnp.int32, (rows, cols), 0)
    c = lax.broadcasted_iota(jnp.int32, (rows, cols), 1)
    return jnp.where(pick(r, c), 1.0, 0.0).astype(BF)


def kernel(
    len_ref, q_ref, k_ref, v_ref, cap_ref, img_ref, w_ref,
    gq_ref, gk_ref, gv_ref, gp_ref,
    kvb, qb, dbuf, cbuf, wsend, wz, wbuf,
    bias, pbuf, lowbuf, dsbuf, p2buf, low2buf, ds2buf, atbuf, dob, lse, delta,
    esend, erecv, gacc, dsend, drecv, csend, crecv, asend, gslot, pick,
    dkown, dvown, dqb, dkb, dvb,
    ssem, rsem, lsem,
):
    dp, seq = lax.axis_index("dp"), lax.axis_index("seq")
    c, x = dp % 2, dp // 8
    y, zl = seq % 4, seq // 4
    z = ((dp // 2) % 4) * 2 + zl
    length = len_ref[0]
    mate_z = device(x, y, z + 1 - 2 * zl, c)
    mate_c = device(x, y, z, 1 - c)
    zh = z // 2
    mirror = device(y, x, z, c)
    on_diagonal = x == y
    off_diagonal = x != y
    count = [0]
    groups = []

    class Group:
        def __init__(self, bulk):
            self.slot, self.bulk = count[0], bulk
            count[0] += 1
            groups.append(self)

        def send(self, src, dst, to):
            pltpu.make_async_remote_copy(
                src_ref=src, dst_ref=dst, send_sem=ssem.at[self.slot], recv_sem=rsem.at[self.slot],
                device_id=to, device_id_type=MESH,
            ).start()
            return self

        def whole(self, bulk):
            return pltpu.make_async_remote_copy(
                src_ref=bulk, dst_ref=bulk, send_sem=ssem.at[self.slot], recv_sem=rsem.at[self.slot],
                device_id=mate_c, device_id_type=MESH,
            )

        def arrive(self):
            self.whole(self.bulk).wait_recv()

        def leave(self):
            self.whole(self.bulk).wait_send()

    def at_x(xx):
        return device(xx % 4, y, z, c)

    def at_y(yy):
        return device(x, yy % 4, z, c)

    def at_z(zz):
        return device(x, y, zz % 8, c)

    def cols(index, width):
        return pl.ds(pl.multiple_of(index * width, 128), width)

    def rows(index, height):
        return pl.ds(pl.multiple_of(index * height, height), height)

    barrier = pltpu.get_barrier_semaphore()

    def greet(to):
        pl.semaphore_signal(barrier, inc=1, device_id=to, device_id_type=MESH)

    for i in range(1, 4):
        greet(at_y(y + i))
        greet(at_x(x + i))
    for i in range(1, 8):
        greet(at_z(z + i))
    greet(mate_c)

    @pl.when(off_diagonal)
    def _():
        greet(mirror)

    for h in range(3):
        lane = cols(y * 3 + h, 128)
        pltpu.make_async_copy(k_ref.at[:, lane], kvb.at[h, 0, y, 0], lsem.at[0]).start()
        pltpu.make_async_copy(v_ref.at[:, lane], kvb.at[h, 0, y, 1], lsem.at[0]).start()
    own_q = pltpu.make_async_copy(q_ref.at[:, cols(y, 384)], qb.at[0, y], lsem.at[1])
    own_d = pltpu.make_async_copy(img_ref, dbuf.at[y, pl.ds(16, 112)], lsem.at[2])
    own_c = pltpu.make_async_copy(cap_ref.at[:, cols(y, 384)], cbuf.at[y], lsem.at[3])
    for cp in (own_q, own_d, own_c):
        cp.start()

    w = jnp.concatenate([w_ref[...].astype(F32), jnp.zeros((2, 1536), F32)], axis=0)
    wsend[...] = jnp.concatenate([w[:, j * 384:(j + 1) * 384] for j in range(4)], axis=0).astype(BF)
    dbuf[:, 0:16, :] = jnp.zeros((4, 16, 1536), BF)

    pl.semaphore_wait(barrier, 14 + off_diagonal.astype(jnp.int32))

    wa = Group(wz.at[0])

    @pl.when(off_diagonal)
    def _():
        wa.send(wsend, wz.at[z], mirror)

    @pl.when(on_diagonal)
    def _():
        wz[z] = wsend[...]

    came = [[] for _ in range(3)]

    def exchange(h):
        for i in (1, 3, 2):
            lane = cols((y + i) % 4 * 3 + h, 128)
            source = (y + 4 - i) % 4
            g = Group(kvb.at[h, 0, source])
            g.send(k_ref.at[:, lane], kvb.at[h, 0, y, 0], at_y(y + i))
            g.send(v_ref.at[:, lane], kvb.at[h, 0, y, 1], at_y(y + i))
            came[h].append((source, g))

    far_kv = [Group(kvb.at[h, 1]) for h in range(3)]
    far_q = [Group(qb.at[1, :, :, pl.ds(h * 128, 128)]) for h in range(3)]

    def pass_kv(h, p):
        far_kv[h].send(kvb.at[h, 0, p], kvb.at[h, 1, p], mate_z)

    def pass_q(h):
        lane = pl.ds(h * 128, 128)
        for i in range(4):
            p = (y + i) % 4
            far_q[h].send(qb.at[0, p, :, lane], qb.at[1, p, :, lane], mate_z)

    near_q = [Group(qb.at[0, pl.ds(0, 3), :, pl.ds(h * 128, 128)]) for h in range(3)]
    mine_d = dbuf.at[y, pl.ds(16, 112)]
    from_low, from_high = Group(mine_d), Group(mine_d)

    def exchange_q(h):
        for i in (1, 3, 2):
            lane = cols((y + i) % 4 * 3 + h, 128)
            near_q[h].send(q_ref.at[:, lane], qb.at[0, y, :, pl.ds(h * 128, 128)], at_y(y + i))

    exchange(0)
    own_kv = kvb.at[pl.ds(0, 3), 0, y]
    pltpu.make_async_copy(own_kv, own_kv, lsem.at[0]).wait()
    for h in range(3):
        pass_kv(h, y)
    exchange(1)
    exchange(2)
    exchange_q(0)
    exchange_q(1)
    own_d.wait()
    from_low.send(mine_d, mine_d, at_y(y + 1))
    from_high.send(mine_d, mine_d, at_y(y + 3))
    exchange_q(2)
    caps = Group(cbuf.at[pl.ds(0, 3)])
    for i in range(1, 4):
        caps.send(cap_ref.at[:, cols((y + i) % 4, 384)], cbuf.at[y], at_y(y + i))

    ki = lax.broadcasted_iota(jnp.int32, (1024, 256), 0)
    blk = jnp.where(ki < 512, zl, 1 - zl) * 4 + (ki // 128) % 4
    off = ki % 128
    bias[...] = jnp.where((off < 16) | (blk * 112 + off - 16 < length), 0.0, NEG)

    for half in range(2):
        pick[half] = select(
            192, 384, lambda r, k: k == r % 48 // 12 * 96 + r % 12 // 6 * 24 + r // 48 * 6 + r % 6 + 48 * half
        )

    @pl.when(off_diagonal)
    def _():
        wa.arrive()

    wc = Group(wz.at[pl.ds(0, 7)])
    for i in (4, 3, 5, 2, 6, 1, 7):
        wc.send(wz.at[z], wz.at[z], at_z(z + i))

    def pass_on(h):
        for p, g in came[h]:
            g.arrive()
            pass_kv(h, p)

    pass_on(0)
    pass_on(1)
    pass_on(2)

    wc.arrive()
    squeeze = select(48, 64, lambda r, k: (k % 8 < 6) & (r == k // 8 * 6 + k % 8))
    for j in range(4):
        padded = jnp.concatenate([wz[i].astype(F32)[j * 8:(j + 1) * 8] for i in range(8)], axis=0).astype(BF)
        wbuf[c, x, j] = dot(squeeze, padded, NN).astype(BF)
    quarter = wbuf.at[c, x]
    wd_low = Group(quarter).send(quarter, quarter, at_x(x + 1))
    wd_high = Group(quarter).send(quarter, quarter, at_x(x + 3))

    def whole(buf, h, which):
        return buf[h, :, :, which].reshape(1024, 128)

    def forward(h):
        lanes = slice(h * 128, (h + 1) * 128)
        far_kv[h].arrive()
        kk, vv = whole(kvb, h, 0), whole(kvb, h, 1)
        for t in range(2):
            part = slice(t * 256, (t + 1) * 256)
            qq = qb[0, 2 * t:2 * t + 2, :, lanes].reshape(256, 128)
            s = dot(kk, qq, NT) + bias[...]
            top = jnp.max(s, axis=0, keepdims=True)
            e = jnp.exp2((s - top) * EXP_SCALE)
            total = jnp.sum(e, axis=0, keepdims=True)
            prob = e * (1.0 / total)
            low = prob.astype(BF)
            pbuf[h, :, part] = prob
            lowbuf[h, :, part] = low
            atbuf[lanes, part] = dot(vv, low, TT).astype(BF)
            lse[0, h:h + 1, part] = top * EXP_SCALE + jnp.log2(total)

    own_q.wait()
    near_q[0].arrive()
    pass_q(0)
    forward(0)
    near_q[1].arrive()
    pass_q(1)
    forward(1)
    from_low.arrive()
    from_both = Group(mine_d)
    piece = dbuf.at[(y + 3) % 4, pl.ds(16, 64)]
    from_both.send(piece, piece, at_y(y + 1))
    from_high.arrive()
    piece = dbuf.at[(y + 1) % 4, pl.ds(80, 48)]
    from_both.send(piece, piece, at_y(y + 3))
    wd_both = Group(quarter)
    wd_low.arrive()
    piece = wbuf.at[c, (x + 3) % 4, pl.ds(0, 2)]
    wd_both.send(piece, piece, at_x(x + 1))
    wd_high.arrive()
    piece = wbuf.at[c, (x + 1) % 4, pl.ds(2, 2)]
    wd_both.send(piece, piece, at_x(x + 3))
    near_q[2].arrive()
    pass_q(2)
    forward(2)
    far_lse = Group(lse.at[1]).send(lse.at[0], lse.at[1], mate_z)
    wd_both.arrive()
    we = Group(wbuf.at[c]).send(wbuf.at[c], wbuf.at[c], mate_c)

    qi = lax.broadcasted_iota(jnp.int32, (384, 512), 1)
    off = qi % 128
    token = (zl * 4 + qi // 128) * 112 + off - 16
    at_image = jnp.where((off >= 16) & (token < length), atbuf[...].astype(F32), 0.0)
    at_image = at_image.astype(BF)

    def features(half):
        return dot(pick[half], at_image, NN).astype(BF)

    own_c.wait()
    caps.arrive()
    from_both.arrive()

    def image_cols(j):
        return dbuf[:, :, j * 384:(j + 1) * 384].reshape(512, 384)

    first = features(1 - c)
    for j in range(4):
        esend[:, :, j * 384:(j + 1) * 384] = dot(first, image_cols(j), NN).astype(BF).reshape(4, 48, 384)
    ge = Group(erecv).send(esend, erecv, mate_c)
    second = features(c)
    for j in range(4):
        gacc[:, :, j * 384:(j + 1) * 384] = dot(second, image_cols(j), NN).reshape(4, 48, 384)

    ge.arrive()
    for j in range(4):
        total = gacc[j] + erecv[j].astype(F32)
        gacc[j] = total
        dsend[j] = total.astype(BF)
    gd = Group(drecv)
    for i in (1, 3, 2):
        gd.send(dsend.at[(x + i) % 4], drecv.at[i - 1], at_x(x + i))

    we.arrive()
    do_all = jnp.zeros((512, 384), F32)
    for j in range(4):
        wj = jnp.concatenate([wbuf[i // 4, i % 4, j] for i in range(8)], axis=0)
        do_all += dot(image_cols(j), wj, NT)
    do_all = dot(do_all.astype(BF), pick[...].reshape(384, 384), NN)
    ri = lax.broadcasted_iota(jnp.int32, (512, 384), 0)
    token = (zl * 4 + ri // 128) * 112 + ri % 128 - 16
    do_all = jnp.where(token < length, do_all, 0.0).astype(BF)
    for h in range(3):
        lanes = slice(h * 128, (h + 1) * 128)
        for p in range(4):
            dob[h, 0, p, 0:16] = cbuf[p, :, lanes]
            dob[h, 0, p, 16:128] = do_all[p * 128 + 16:(p + 1) * 128, lanes]
        for t in range(2):
            part = slice(t * 256, (t + 1) * 256)
            do = dob[h, 0, 2 * t:2 * t + 2].reshape(256, 128)
            delta[0, h:h + 1, part] = jnp.sum(
                do.astype(F32).T * atbuf[lanes, part].astype(F32), axis=0, keepdims=True
            )
    far_delta = Group(delta.at[1]).send(delta.at[0], delta.at[1], mate_z)
    far_do = [Group(dob.at[h, 1]).send(dob.at[h, 0], dob.at[h, 1], mate_z) for h in range(3)]

    outs = [(Group(ref.at[:, pl.ds(0, 1152)]), ref, 4 + i) for i, ref in enumerate((gq_ref, gk_ref, gv_ref))]

    def to_rows(src, which, h):
        group, out, sem = outs[which]
        lane = cols(y * 3 + h, 128)
        for i in (1, 3, 2):
            group.send(src.at[h, rows((y + i) % 4, 128)], out.at[:, lane], at_y(y + i))
        pltpu.make_async_copy(src.at[h, rows(y, 128)], out.at[:, lane], lsem.at[sem]).start()

    def backward(h):
        kk, vv = whole(kvb, h, 0), whole(kvb, h, 1)
        for t in range(2):
            part = slice(t * 256, (t + 1) * 256)
            do = dob[h, 0, 2 * t:2 * t + 2].reshape(256, 128)
            dsbuf[:, part] = (pbuf[h, :, part] * (dot(vv, do, NT) - delta[0, h:h + 1, part])).astype(BF)
        dqb[h] = (dot(kk, dsbuf[...], TT) * SCALE).T.astype(BF)
        to_rows(dqb, 0, h)
        lanes = slice(h * 128, (h + 1) * 128)
        dvown[h] = dot(lowbuf[h, 0:512], dob[h, 0].reshape(512, 128), NN)
        dkown[h] = dot(dsbuf[0:512], qb[0, :, :, lanes].reshape(512, 128), NN)

    def far_probs(h):
        lanes = slice(h * 128, (h + 1) * 128)
        kk = kvb[h, 0, :, 0].reshape(512, 128)
        for t in range(2):
            part = slice(t * 256, (t + 1) * 256)
            s = dot(kk, qb[1, 2 * t:2 * t + 2, :, lanes].reshape(256, 128), NT) + bias[0:512]
            prob = jnp.exp2(s * EXP_SCALE - lse[1, h:h + 1, part])
            p2buf[h, :, part] = prob
            low2buf[h, :, part] = prob.astype(BF)

    def far_backward(h):
        lanes = slice(h * 128, (h + 1) * 128)
        far_do[h].arrive()
        vv = kvb[h, 0, :, 1].reshape(512, 128)
        for t in range(2):
            part = slice(t * 256, (t + 1) * 256)
            do = dob[h, 1, 2 * t:2 * t + 2].reshape(256, 128)
            ds2buf[:, part] = (p2buf[h, :, part] * (dot(vv, do, NT) - delta[1, h:h + 1, part])).astype(BF)
        far_qq = qb[1, :, :, lanes].reshape(512, 128)
        dkb[h] = ((dkown[h] + dot(ds2buf[...], far_qq, NN)) * SCALE).astype(BF)
        to_rows(dkb, 1, h)
        dvb[h] = (dvown[h] + dot(low2buf[h], dob[h, 1].reshape(512, 128), NN)).astype(BF)
        to_rows(dvb, 2, h)

    backward(0)
    backward(1)
    backward(2)
    far_lse.arrive()
    for h in range(3):
        far_q[h].arrive()
        far_probs(h)
    far_delta.arrive()
    far_backward(0)
    far_backward(1)

    gd.arrive()
    total = gacc[x] + drecv[0].astype(F32) + drecv[1].astype(F32) + drecv[2].astype(F32)
    spread = select(64, 48, lambda r, k: (r % 8 < 6) & (k == r // 8 * 6 + r % 8))
    total = dot(spread, total.astype(BF), NN)
    for zz in range(8):
        csend[zz] = jnp.concatenate(
            [total[zz * 8:(zz + 1) * 8, j * 384:(j + 1) * 384] for j in range(4)], axis=0
        ).astype(BF)
    gc = Group(crecv)
    for i in (4, 3, 5, 2, 6, 1, 7):
        gc.send(csend.at[(z + i) % 8], crecv.at[i - 1], at_z(z + i))
    far_backward(2)

    gc.arrive()
    total = csend[z].astype(F32)
    for i in range(7):
        total += crecv[i].astype(F32)
    asend[...] = total
    ga = Group(gslot)

    @pl.when(off_diagonal)
    def _():
        ga.send(asend, gslot, mirror)

    @pl.when(on_diagonal)
    def _():
        gslot[...] = total

    for group, out, sem in outs:
        group.arrive()
        bulk = out.at[:, pl.ds(0, 384)]
        pltpu.make_async_copy(bulk, bulk, lsem.at[sem]).wait()
    for group in groups:
        if group not in (wa, ga):
            group.leave()

    @pl.when(off_diagonal)
    def _():
        wa.leave()
        ga.leave()
        ga.arrive()

    for j in range(4):
        gp_ref[:, j * 384:(j + 1) * 384] = gslot[j * 8:j * 8 + 6]
    assert count[0] == SEMS


def copy_out(a, b, c, d, a_out, b_out, c_out, d_out, a_buf, b_buf, c_buf, d_buf, sem):
    chains = ((a, a_buf, a_out), (b, b_buf, b_out), (c, c_buf, c_out), (d, d_buf, d_out))
    reads = [pltpu.make_async_copy(src, buf, sem.at[i]) for i, (src, buf, _) in enumerate(chains)]
    writes = [pltpu.make_async_copy(buf, dst, sem.at[4 + i]) for i, (_, buf, dst) in enumerate(chains)]
    for cp in reads:
        cp.start()
    for read, write in zip(reads, writes):
        read.wait()
        write.start()
    for cp in writes:
        cp.wait()


def shards(query_rows, key_rows, value_rows, d_caption, d_image, proj_weight, lengths):
    block = jax.ShapeDtypeStruct((128, 1536), BF)
    outs = (block, block, block, jax.ShapeDtypeStruct((6, 1536), F32))
    hbm = pl.BlockSpec(memory_space=pl.ANY)
    vmem = pl.BlockSpec(memory_space=pltpu.VMEM)
    scratch = [
        pltpu.VMEM(shape, dtype)
        for shape, dtype in (
            ((3, 2, 4, 2, 128, 128), BF), ((2, 4, 128, 384), BF), ((4, 128, 1536), BF), ((4, 16, 384), BF),
            ((32, 384), BF), ((8, 32, 384), BF), ((2, 4, 4, 48, 384), BF),
            ((1024, 256), F32), ((3, 1024, 512), F32), ((3, 1024, 512), BF), ((1024, 512), BF),
            ((3, 512, 512), F32), ((3, 512, 512), BF), ((512, 512), BF),
            ((384, 512), BF), ((3, 2, 4, 128, 128), BF), ((2, 8, 512), F32), ((2, 8, 512), F32),
            ((4, 48, 1536), BF), ((4, 48, 1536), BF), ((4, 48, 1536), F32), ((4, 48, 1536), BF),
            ((3, 48, 1536), BF), ((8, 32, 384), BF), ((7, 32, 384), BF), ((32, 384), F32), ((32, 384), F32), ((2, 192, 384), BF),
            ((3, 512, 128), F32), ((3, 512, 128), F32),
            ((3, 512, 128), BF), ((3, 512, 128), BF), ((3, 512, 128), BF),
        )
    ]
    results = pl.pallas_call(
        kernel,
        out_shape=outs,
        in_specs=[pl.BlockSpec(memory_space=pltpu.SMEM), hbm, hbm, hbm, hbm, hbm, vmem],
        out_specs=(hbm, hbm, hbm, vmem),
        scratch_shapes=scratch + [
            pltpu.SemaphoreType.DMA((SEMS,)), pltpu.SemaphoreType.DMA((SEMS,)), pltpu.SemaphoreType.DMA((LOCALS,)),
        ],
        compiler_params=pltpu.CompilerParams(
            collective_id=0, has_side_effects=True, vmem_limit_bytes=56 * 2**20
        ),
        name="joint_attention_backward",
    )(lengths, query_rows, key_rows, value_rows, d_caption, d_image, proj_weight)
    return pl.pallas_call(
        copy_out,
        out_shape=outs,
        in_specs=[hbm] * 4,
        out_specs=(hbm,) * 4,
        scratch_shapes=[pltpu.VMEM(o.shape, o.dtype) for o in outs] + [pltpu.SemaphoreType.DMA((8,))],
        name="copy_out",
    )(*results)


def solution(mesh):
    placed = P(("dp", "seq"), None)
    return jax.shard_map(
        shards,
        mesh=mesh,
        in_specs=(placed,) * 6 + (P("dp"),),
        out_specs=(placed,) * 4,
        check_vma=False,
    )
```

time: 71 us -> 66.7 us (0.939)
  the two profiles are of different devices: /device:TPU:4 before, /device:TPU:25 now
where the time goes in v3:
time: 66.7 us; the launch traced here: 66.5 us
  Pallas kernels  65.2 us (98%)
  between operations  1.29 us (2%)
    pallas_call x1, Pallas kernels, shards(): pl.pallas_call(kernel, out_shape=outs, in_specs=[pl.BlockSpec(memory_spac...  63.1 us
    pallas_call x1, Pallas kernels, shards(): pl.pallas_call(copy_out, out_shape=outs, in_specs=[hbm] * 4, out_specs=(h...  2.07 us

profile of v3, /device:TPU:25, one launch (start us, length us, event | category | flops | bytes accessed | tf_op | source)
XLA Modules:
  0.0 66.5 jit_solution(16267295531535274516)
XLA Ops:
  1.3 63.1 %joint_attention_backward.1 = (bf16[128,1536]{1,0:T(8,128)(2,1)}, bf16[128,1536]{1,0:T(8,128)(2,1)}, bf16[128,1536]{1,0:T(8,128)(2,1)}, f32[6,1536]{1,0:T(8,128)}) custom-call(s32[1]{0:T(128)S(6)} %copy.11.len_ref, bf16[128,1536]{1,0:T(8,128)(2,1)} %q_ref.1, bf16[128,1536]{1,0:T(8,128)(2,1)} %k_ref.1, bf16[128,1536]{1,0:T(8,128)(2,1)} %v_ref.1, ...), custom_call_target="tpu_custom_call" | custom-call | tf_op jit(solution)/shard_map/joint_attention_backward/pallas_call | solution.py:463
  64.4 2.1 %copy_out.1 = (bf16[128,1536]{1,0:T(8,128)(2,1)}, bf16[128,1536]{1,0:T(8,128)(2,1)}, bf16[128,1536]{1,0:T(8,128)(2,1)}, f32[6,1536]{1,0:T(8,128)}) custom-call(bf16[128,1536]{1,0:T(8,128)(2,1)} %get-tuple-element.8.a, bf16[128,1536]{1,0:T(8,128)(2,1)} %get-tuple-element.9.b, bf16[128,1536]{1,0:T(8,128)(2,1)} %get-tuple-element.10.c, ...), custom_call_target="tpu_custom_call" | custom-call | tf_op jit(solution)/shard_map/copy_out/pallas_call | solution.py:476

commit v4 on v3

--- a/solution.py
+++ b/solution.py
@@ -13,7 +13,7 @@
 NT = (((1,), (1,)), ((), ()))
 TT = (((0,), (0,)), ((), ()))
 NN = (((1,), (0,)), ((), ()))
-SEMS, LOCALS = 40, 7
+SEMS, LOCALS = 44, 9
 
 
 def dot(a, b, dims):
@@ -33,9 +33,9 @@
 def kernel(
     len_ref, q_ref, k_ref, v_ref, cap_ref, img_ref, w_ref,
     gq_ref, gk_ref, gv_ref, gp_ref,
-    kvb, qb, dbuf, cbuf, wsend, wz, wbuf,
+    kvb, qb, dbuf, cbuf, wbuf6, wsend, wz, wbuf,
     bias, pbuf, lowbuf, dsbuf, p2buf, low2buf, ds2buf, atbuf, dob, lse, delta,
-    esend, erecv, gacc, dsend, drecv, csend, crecv, asend, gslot, pick,
+    esend, erecv, gacc, dsend, drecv, csend, crecv, asend, pick,
     dkown, dvown, dqb, dkb, dvb,
     ssem, rsem, lsem,
 ):
@@ -47,7 +47,9 @@
     mate_z = device(x, y, z + 1 - 2 * zl, c)
     mate_c = device(x, y, z, 1 - c)
     zh = z // 2
+    outer_z = device(x, y, (z + 7 + 2 * zl) % 8, c)
     mirror = device(y, x, z, c)
+    zh = z // 2
     on_diagonal = x == y
     off_diagonal = x != y
     count = [0]
@@ -109,6 +111,8 @@
     def _():
         greet(mirror)
 
+    own_w = pltpu.make_async_copy(w_ref, wbuf6, lsem.at[7])
+    own_w.start()
     for h in range(3):
         lane = cols(y * 3 + h, 128)
         pltpu.make_async_copy(k_ref.at[:, lane], kvb.at[h, 0, y, 0], lsem.at[0]).start()
@@ -119,21 +123,22 @@
     for cp in (own_q, own_d, own_c):
         cp.start()
 
-    w = jnp.concatenate([w_ref[...].astype(F32), jnp.zeros((2, 1536), F32)], axis=0)
+    dbuf[:, 0:16, :] = jnp.zeros((4, 16, 1536), BF)
+
+    pl.semaphore_wait(barrier, 14 + off_diagonal.astype(jnp.int32))
+
+    own_w.wait()
+    w = jnp.concatenate([wbuf6[...].astype(F32), jnp.zeros((2, 1536), F32)], axis=0)
     wsend[...] = jnp.concatenate([w[:, j * 384:(j + 1) * 384] for j in range(4)], axis=0).astype(BF)
-    dbuf[:, 0:16, :] = jnp.zeros((4, 16, 1536), BF)
-
-    pl.semaphore_wait(barrier, 14 + off_diagonal.astype(jnp.int32))
-
-    wa = Group(wz.at[0])
+    wa = Group(wz.at[0, 0])
 
     @pl.when(off_diagonal)
     def _():
-        wa.send(wsend, wz.at[z], mirror)
+        wa.send(wsend, wz.at[zl, zh], mirror)
 
     @pl.when(on_diagonal)
     def _():
-        wz[z] = wsend[...]
+        wz[zl, zh] = wsend[...]
 
     came = [[] for _ in range(3)]
 
@@ -198,9 +203,9 @@
     def _():
         wa.arrive()
 
-    wc = Group(wz.at[pl.ds(0, 7)])
-    for i in (4, 3, 5, 2, 6, 1, 7):
-        wc.send(wz.at[z], wz.at[z], at_z(z + i))
+    wc = Group(wz.at[0, pl.ds(0, 3)])
+    for i in (2, 1, 3):
+        wc.send(wz.at[zl, zh], wz.at[zl, zh], at_z(z + 2 * i))
 
     def pass_on(h):
         for p, g in came[h]:
@@ -209,13 +214,15 @@
 
     pass_on(0)
     pass_on(1)
+    wc.arrive()
+    wc_outer = Group(wz.at[0]).send(wz.at[zl], wz.at[zl], outer_z)
     pass_on(2)
 
-    wc.arrive()
+    wc_outer.arrive()
     squeeze = select(48, 64, lambda r, k: (k % 8 < 6) & (r == k // 8 * 6 + k % 8))
     for j in range(4):
-        padded = jnp.concatenate([wz[i].astype(F32)[j * 8:(j + 1) * 8] for i in range(8)], axis=0).astype(BF)
-        wbuf[c, x, j] = dot(squeeze, padded, NN).astype(BF)
+        padded = jnp.concatenate([wz[i % 2, i // 2].astype(F32)[j * 8:(j + 1) * 8] for i in range(8)], axis=0).astype(BF)
+        wbuf[c, x, :, j * 384:(j + 1) * 384] = dot(squeeze, padded, NN).astype(BF)
     quarter = wbuf.at[c, x]
     wd_low = Group(quarter).send(quarter, quarter, at_x(x + 1))
     wd_high = Group(quarter).send(quarter, quarter, at_x(x + 3))
@@ -248,6 +255,13 @@
     near_q[1].arrive()
     pass_q(1)
     forward(1)
+    wd_both = Group(quarter)
+    wd_low.arrive()
+    piece = wbuf.at[c, (x + 3) % 4, :, pl.ds(0, 768)]
+    wd_both.send(piece, piece, at_x(x + 1))
+    wd_high.arrive()
+    piece = wbuf.at[c, (x + 1) % 4, :, pl.ds(768, 768)]
+    wd_both.send(piece, piece, at_x(x + 3))
     from_low.arrive()
     from_both = Group(mine_d)
     piece = dbuf.at[(y + 3) % 4, pl.ds(16, 64)]
@@ -255,19 +269,38 @@
     from_high.arrive()
     piece = dbuf.at[(y + 1) % 4, pl.ds(80, 48)]
     from_both.send(piece, piece, at_y(y + 3))
-    wd_both = Group(quarter)
-    wd_low.arrive()
-    piece = wbuf.at[c, (x + 3) % 4, pl.ds(0, 2)]
-    wd_both.send(piece, piece, at_x(x + 1))
-    wd_high.arrive()
-    piece = wbuf.at[c, (x + 1) % 4, pl.ds(2, 2)]
-    wd_both.send(piece, piece, at_x(x + 3))
+    wd_both.arrive()
+    we = Group(wbuf.at[c]).send(wbuf.at[c], wbuf.at[c], mate_c)
     near_q[2].arrive()
     pass_q(2)
     forward(2)
     far_lse = Group(lse.at[1]).send(lse.at[0], lse.at[1], mate_z)
-    wd_both.arrive()
-    we = Group(wbuf.at[c]).send(wbuf.at[c], wbuf.at[c], mate_c)
+
+    far_do = [Group(dob.at[h, 1]) for h in range(3)]
+    caps.arrive()
+    own_c.wait()
+    we.arrive()
+
+    def cotangents(places):
+        image = jnp.concatenate([dbuf[p] for p in places], axis=0)
+        total = dot(image, wbuf[...].reshape(384, 1536), NT)
+        total = dot(total.astype(BF), pick[...].reshape(384, 384), NN)
+        off = lax.broadcasted_iota(jnp.int32, (128, 384), 0)
+        for n, p in enumerate(places):
+            token = (zl * 4 + p) * 112 + off - 16
+            part = jnp.where(token < length, total[n * 128:(n + 1) * 128], 0.0).astype(BF)
+            for h in range(3):
+                lanes = slice(h * 128, (h + 1) * 128)
+                dob[h, 0, p, 0:16] = cbuf[p, :, lanes]
+                dob[h, 0, p, 16:128] = part[16:128, lanes]
+
+    def pass_do(h, p):
+        far_do[h].send(dob.at[h, 0, p], dob.at[h, 1, p], mate_z)
+
+    cotangents([y, (y + 1) % 4, (y + 3) % 4])
+    for h in range(2):
+        for i in (0, 1, 3):
+            pass_do(h, (y + i) % 4)
 
     qi = lax.broadcasted_iota(jnp.int32, (384, 512), 1)
     off = qi % 128
@@ -278,44 +311,37 @@
     def features(half):
         return dot(pick[half], at_image, NN).astype(BF)
 
-    own_c.wait()
-    caps.arrive()
+    halves = (slice(0, 768), slice(768, 1536))
+
+    def project(kept, out, part):
+        image = dbuf[:, :, part].reshape(512, 768)
+        out[:, :, part] = dot(kept, image, NN).astype(out.dtype).reshape(4, 48, 768)
+
+    kept_far, kept_own = features(1 - c), features(c)
     from_both.arrive()
 
-    def image_cols(j):
-        return dbuf[:, :, j * 384:(j + 1) * 384].reshape(512, 384)
-
-    first = features(1 - c)
-    for j in range(4):
-        esend[:, :, j * 384:(j + 1) * 384] = dot(first, image_cols(j), NN).astype(BF).reshape(4, 48, 384)
-    ge = Group(erecv).send(esend, erecv, mate_c)
-    second = features(c)
-    for j in range(4):
-        gacc[:, :, j * 384:(j + 1) * 384] = dot(second, image_cols(j), NN).reshape(4, 48, 384)
-
-    ge.arrive()
-    for j in range(4):
-        total = gacc[j] + erecv[j].astype(F32)
-        gacc[j] = total
-        dsend[j] = total.astype(BF)
-    gd = Group(drecv)
-    for i in (1, 3, 2):
-        gd.send(dsend.at[(x + i) % 4], drecv.at[i - 1], at_x(x + i))
-
-    we.arrive()
-    do_all = jnp.zeros((512, 384), F32)
-    for j in range(4):
-        wj = jnp.concatenate([wbuf[i // 4, i % 4, j] for i in range(8)], axis=0)
-        do_all += dot(image_cols(j), wj, NT)
-    do_all = dot(do_all.astype(BF), pick[...].reshape(384, 384), NN)
-    ri = lax.broadcasted_iota(jnp.int32, (512, 384), 0)
-    token = (zl * 4 + ri // 128) * 112 + ri % 128 - 16
-    do_all = jnp.where(token < length, do_all, 0.0).astype(BF)
+    ge = []
+    for part in halves:
+        project(kept_far, esend, part)
+        lanes = pl.ds(part.start, 768)
+        ge.append(Group(erecv.at[:, :, lanes]).send(esend.at[:, :, lanes], erecv.at[:, :, lanes], mate_c))
+    for part in halves:
+        project(kept_own, gacc, part)
+    gd = []
+    for part, half in zip(halves, ge):
+        half.arrive()
+        total = gacc[:, :, part] + erecv[:, :, part].astype(F32)
+        gacc[:, :, part] = total
+        dsend[:, :, part] = total.astype(BF)
+        lanes = pl.ds(part.start, 768)
+        gd.append(Group(drecv.at[:, :, lanes]))
+        for i in (1, 3, 2):
+            gd[-1].send(dsend.at[(x + i) % 4, :, lanes], drecv.at[i - 1, :, lanes], at_x(x + i))
+
+    cotangents([(y + 2) % 4])
+
     for h in range(3):
         lanes = slice(h * 128, (h + 1) * 128)
-        for p in range(4):
-            dob[h, 0, p, 0:16] = cbuf[p, :, lanes]
-            dob[h, 0, p, 16:128] = do_all[p * 128 + 16:(p + 1) * 128, lanes]
         for t in range(2):
             part = slice(t * 256, (t + 1) * 256)
             do = dob[h, 0, 2 * t:2 * t + 2].reshape(256, 128)
@@ -323,7 +349,9 @@
                 do.astype(F32).T * atbuf[lanes, part].astype(F32), axis=0, keepdims=True
             )
     far_delta = Group(delta.at[1]).send(delta.at[0], delta.at[1], mate_z)
-    far_do = [Group(dob.at[h, 1]).send(dob.at[h, 0], dob.at[h, 1], mate_z) for h in range(3)]
+    for h in range(2):
+        pass_do(h, (y + 2) % 4)
+    far_do[2].send(dob.at[2, 0], dob.at[2, 1], mate_z)
 
     outs = [(Group(ref.at[:, pl.ds(0, 1152)]), ref, 4 + i) for i, ref in enumerate((gq_ref, gk_ref, gv_ref))]
 
@@ -379,35 +407,45 @@
         far_probs(h)
     far_delta.arrive()
     far_backward(0)
+
+    spread = select(64, 48, lambda r, k: (r % 8 < 6) & (k == r // 8 * 6 + r % 8))
+    gc = []
+
+    def along_z(n):
+        gd[n].arrive()
+        part = halves[n]
+        total = gacc[x, :, part]
+        for i in range(3):
+            total += drecv[i, :, part].astype(F32)
+        total = dot(spread, total.astype(BF), NN)
+        for zz in range(8):
+            rows_z = total[zz * 8:(zz + 1) * 8]
+            csend[zz, n] = jnp.concatenate([rows_z[:, 0:384], rows_z[:, 384:768]], axis=0).astype(BF)
+        gc.append(Group(crecv.at[:, n]))
+        for i in (4, 3, 5, 2, 6, 1, 7):
+            gc[n].send(csend.at[(z + i) % 8, n], crecv.at[i - 1, n], at_z(z + i))
+
+    along_z(0)
     far_backward(1)
-
-    gd.arrive()
-    total = gacc[x] + drecv[0].astype(F32) + drecv[1].astype(F32) + drecv[2].astype(F32)
-    spread = select(64, 48, lambda r, k: (r % 8 < 6) & (k == r // 8 * 6 + r % 8))
-    total = dot(spread, total.astype(BF), NN)
-    for zz in range(8):
-        csend[zz] = jnp.concatenate(
-            [total[zz * 8:(zz + 1) * 8, j * 384:(j + 1) * 384] for j in range(4)], axis=0
-        ).astype(BF)
-    gc = Group(crecv)
-    for i in (4, 3, 5, 2, 6, 1, 7):
-        gc.send(csend.at[(z + i) % 8], crecv.at[i - 1], at_z(z + i))
     far_backward(2)
-
-    gc.arrive()
+    along_z(1)
+
+    for group in gc:
+        group.arrive()
     total = csend[z].astype(F32)
     for i in range(7):
         total += crecv[i].astype(F32)
-    asend[...] = total
-    ga = Group(gslot)
+    total = total.reshape(32, 384)
+    asend[...] = total.astype(BF)
+    ga = Group(gp_ref)
 
     @pl.when(off_diagonal)
     def _():
-        ga.send(asend, gslot, mirror)
+        ga.send(asend, gp_ref, mirror)
 
     @pl.when(on_diagonal)
     def _():
-        gslot[...] = total
+        pltpu.make_async_copy(asend, gp_ref, lsem.at[8]).start()
 
     for group, out, sem in outs:
         group.arrive()
@@ -423,17 +461,28 @@
         ga.leave()
         ga.arrive()
 
-    for j in range(4):
-        gp_ref[:, j * 384:(j + 1) * 384] = gslot[j * 8:j * 8 + 6]
+    @pl.when(on_diagonal)
+    def _():
+        pltpu.make_async_copy(asend, gp_ref, lsem.at[8]).wait()
+
     assert count[0] == SEMS
 
 
-def copy_out(a, b, c, d, a_out, b_out, c_out, d_out, a_buf, b_buf, c_buf, d_buf, sem):
-    chains = ((a, a_buf, a_out), (b, b_buf, b_out), (c, c_buf, c_out), (d, d_buf, d_out))
-    reads = [pltpu.make_async_copy(src, buf, sem.at[i]) for i, (src, buf, _) in enumerate(chains)]
-    writes = [pltpu.make_async_copy(buf, dst, sem.at[4 + i]) for i, (_, buf, dst) in enumerate(chains)]
+def copy_out(gq, gk, gv, gp, gq_out, gk_out, gv_out, gp_out, buf, gp_in, sem):
+    small = pltpu.make_async_copy(gp, gp_in, sem.at[0])
+    small.start()
+    pieces = [(n, h, src, dst) for h in range(2) for n, (src, dst) in enumerate(((gq, gq_out), (gk, gk_out), (gv, gv_out)))]
+    reads, writes = [], []
+    for n, h, src, dst in pieces:
+        rows, k = pl.ds(h * 64, 64), 1 + 2 * n + h
+        reads.append(pltpu.make_async_copy(src.at[rows], buf.at[n, rows], sem.at[k]))
+        writes.append(pltpu.make_async_copy(buf.at[n, rows], dst.at[rows], sem.at[6 + k]))
     for cp in reads:
         cp.start()
+    small.wait()
+    rows = gp_in[...].astype(F32)
+    for j in range(4):
+        gp_out[:, j * 384:(j + 1) * 384] = rows[j * 8:j * 8 + 6]
     for read, write in zip(reads, writes):
         read.wait()
         write.start()
@@ -450,21 +499,21 @@
         pltpu.VMEM(shape, dtype)
         for shape, dtype in (
             ((3, 2, 4, 2, 128, 128), BF), ((2, 4, 128, 384), BF), ((4, 128, 1536), BF), ((4, 16, 384), BF),
-            ((32, 384), BF), ((8, 32, 384), BF), ((2, 4, 4, 48, 384), BF),
+            ((6, 1536), BF), ((32, 384), BF), ((2, 4, 32, 384), BF), ((2, 4, 48, 1536), BF),
             ((1024, 256), F32), ((3, 1024, 512), F32), ((3, 1024, 512), BF), ((1024, 512), BF),
             ((3, 512, 512), F32), ((3, 512, 512), BF), ((512, 512), BF),
             ((384, 512), BF), ((3, 2, 4, 128, 128), BF), ((2, 8, 512), F32), ((2, 8, 512), F32),
             ((4, 48, 1536), BF), ((4, 48, 1536), BF), ((4, 48, 1536), F32), ((4, 48, 1536), BF),
-            ((3, 48, 1536), BF), ((8, 32, 384), BF), ((7, 32, 384), BF), ((32, 384), F32), ((32, 384), F32), ((2, 192, 384), BF),
+            ((3, 48, 1536), BF), ((8, 2, 16, 384), BF), ((7, 2, 16, 384), BF), ((32, 384), BF), ((2, 192, 384), BF),
             ((3, 512, 128), F32), ((3, 512, 128), F32),
             ((3, 512, 128), BF), ((3, 512, 128), BF), ((3, 512, 128), BF),
         )
     ]
     results = pl.pallas_call(
         kernel,
-        out_shape=outs,
-        in_specs=[pl.BlockSpec(memory_space=pltpu.SMEM), hbm, hbm, hbm, hbm, hbm, vmem],
-        out_specs=(hbm, hbm, hbm, vmem),
+        out_shape=(block, block, block, jax.ShapeDtypeStruct((32, 384), BF)),
+        in_specs=[pl.BlockSpec(memory_space=pltpu.SMEM), hbm, hbm, hbm, hbm, hbm, hbm],
+        out_specs=(hbm,) * 4,
         scratch_shapes=scratch + [
             pltpu.SemaphoreType.DMA((SEMS,)), pltpu.SemaphoreType.DMA((SEMS,)), pltpu.SemaphoreType.DMA((LOCALS,)),
         ],
@@ -477,8 +526,10 @@
         copy_out,
         out_shape=outs,
         in_specs=[hbm] * 4,
-        out_specs=(hbm,) * 4,
-        scratch_shapes=[pltpu.VMEM(o.shape, o.dtype) for o in outs] + [pltpu.SemaphoreType.DMA((8,))],
+        out_specs=(hbm, hbm, hbm, vmem),
+        scratch_shapes=[
+            pltpu.VMEM((3, 128, 1536), BF), pltpu.VMEM((32, 384), BF), pltpu.SemaphoreType.DMA((13,)),
+        ],
         name="copy_out",
     )(*results)
 

time: 66.7 us -> 62.6 us (0.939)
  the two profiles are of different devices: /device:TPU:25 before, /device:TPU:4 now
where the time goes in v4:
time: 62.6 us; the launch traced here: 62.5 us
  Pallas kernels  61.2 us (98%)
  between operations  1.29 us (2%)
    pallas_call x1, Pallas kernels, shards(): pl.pallas_call(kernel, out_shape=(block, block, block, jax.ShapeDtypeStru...  58.5 us
    pallas_call x1, Pallas kernels, shards(): pl.pallas_call(copy_out, out_shape=outs, in_specs=[hbm] * 4, out_specs=(h...  2.77 us

profile of v4, /device:TPU:4, one launch (start us, length us, event | category | flops | bytes accessed | tf_op | source)
XLA Modules:
  0.0 62.5 jit_solution(7016805402310865605)
XLA Ops:
  1.3 58.5 %joint_attention_backward.1 = (bf16[128,1536]{1,0:T(8,128)(2,1)}, bf16[128,1536]{1,0:T(8,128)(2,1)}, bf16[128,1536]{1,0:T(8,128)(2,1)}, bf16[32,384]{1,0:T(8,128)(2,1)}) custom-call(s32[1]{0:T(128)S(6)} %copy.11.len_ref, bf16[128,1536]{1,0:T(8,128)(2,1)} %q_ref.1, bf16[128,1536]{1,0:T(8,128)(2,1)} %k_ref.1, bf16[128,1536]{1,0:T(8,128)(2,1)} %v_ref.1, ...), custom_call_target="tpu_custom_call" | custom-call | tf_op jit(solution)/shard_map/joint_attention_backward/pallas_call | solution.py:512
  59.8 2.8 %copy_out.1 = (bf16[128,1536]{1,0:T(8,128)(2,1)}, bf16[128,1536]{1,0:T(8,128)(2,1)}, bf16[128,1536]{1,0:T(8,128)(2,1)}, f32[6,1536]{1,0:T(8,128)}) custom-call(bf16[128,1536]{1,0:T(8,128)(2,1)} %get-tuple-element.8.gq, bf16[128,1536]{1,0:T(8,128)(2,1)} %get-tuple-element.9.gk, bf16[128,1536]{1,0:T(8,128)(2,1)} %get-tuple-element.10.gv, ...), custom_call_target="tpu_custom_call" | custom-call | tf_op jit(solution)/shard_map/copy_out/pallas_call | solution.py:525

commit v5 on v4

--- a/solution.py
+++ b/solution.py
@@ -13,7 +13,7 @@
 NT = (((1,), (1,)), ((), ()))
 TT = (((0,), (0,)), ((), ()))
 NN = (((1,), (0,)), ((), ()))
-SEMS, LOCALS = 44, 9
+SEMS, LOCALS = 44, 10
 
 
 def dot(a, b, dims):
@@ -33,7 +33,7 @@
 def kernel(
     len_ref, q_ref, k_ref, v_ref, cap_ref, img_ref, w_ref,
     gq_ref, gk_ref, gv_ref, gp_ref,
-    kvb, qb, dbuf, cbuf, wbuf6, wsend, wz, wbuf,
+    len_buf, kvb, qb, dbuf, cbuf, wbuf6, wsend, wz, wbuf,
     bias, pbuf, lowbuf, dsbuf, p2buf, low2buf, ds2buf, atbuf, dob, lse, delta,
     esend, erecv, gacc, dsend, drecv, csend, crecv, asend, pick,
     dkown, dvown, dqb, dkb, dvb,
@@ -43,7 +43,6 @@
     c, x = dp % 2, dp // 8
     y, zl = seq % 4, seq // 4
     z = ((dp // 2) % 4) * 2 + zl
-    length = len_ref[0]
     mate_z = device(x, y, z + 1 - 2 * zl, c)
     mate_c = device(x, y, z, 1 - c)
     zh = z // 2
@@ -111,6 +110,8 @@
     def _():
         greet(mirror)
 
+    own_len = pltpu.make_async_copy(len_ref, len_buf, lsem.at[9])
+    own_len.start()
     own_w = pltpu.make_async_copy(w_ref, wbuf6, lsem.at[7])
     own_w.start()
     for h in range(3):
@@ -189,6 +190,8 @@
     for i in range(1, 4):
         caps.send(cap_ref.at[:, cols((y + i) % 4, 384)], cbuf.at[y], at_y(y + i))
 
+    own_len.wait()
+    length = len_buf[0]
     ki = lax.broadcasted_iota(jnp.int32, (1024, 256), 0)
     blk = jnp.where(ki < 512, zl, 1 - zl) * 4 + (ki // 128) % 4
     off = ki % 128
@@ -468,24 +471,17 @@
     assert count[0] == SEMS
 
 
-def copy_out(gq, gk, gv, gp, gq_out, gk_out, gv_out, gp_out, buf, gp_in, sem):
-    small = pltpu.make_async_copy(gp, gp_in, sem.at[0])
-    small.start()
-    pieces = [(n, h, src, dst) for h in range(2) for n, (src, dst) in enumerate(((gq, gq_out), (gk, gk_out), (gv, gv_out)))]
-    reads, writes = [], []
-    for n, h, src, dst in pieces:
-        rows, k = pl.ds(h * 64, 64), 1 + 2 * n + h
-        reads.append(pltpu.make_async_copy(src.at[rows], buf.at[n, rows], sem.at[k]))
-        writes.append(pltpu.make_async_copy(buf.at[n, rows], dst.at[rows], sem.at[6 + k]))
-    for cp in reads:
+def copy_out(gq, gk, gv, gp, gq_out, gk_out, gv_out, gp_out, gp_buf, sem):
+    writes = [
+        pltpu.make_async_copy(src, dst, sem.at[n])
+        for n, (src, dst) in enumerate(((gq, gq_out), (gk, gk_out), (gv, gv_out), (gp_buf, gp_out)))
+    ]
+    for cp in writes[:3]:
         cp.start()
-    small.wait()
-    rows = gp_in[...].astype(F32)
+    rows = gp[...].astype(F32)
     for j in range(4):
-        gp_out[:, j * 384:(j + 1) * 384] = rows[j * 8:j * 8 + 6]
-    for read, write in zip(reads, writes):
-        read.wait()
-        write.start()
+        gp_buf[:, j * 384:(j + 1) * 384] = rows[j * 8:j * 8 + 6]
+    writes[3].start()
     for cp in writes:
         cp.wait()
 
@@ -511,10 +507,10 @@
     ]
     results = pl.pallas_call(
         kernel,
-        out_shape=(block, block, block, jax.ShapeDtypeStruct((32, 384), BF)),
-        in_specs=[pl.BlockSpec(memory_space=pltpu.SMEM), hbm, hbm, hbm, hbm, hbm, hbm],
-        out_specs=(hbm,) * 4,
-        scratch_shapes=scratch + [
+        out_shape=(pltpu.VMEM((128, 1536), BF),) * 3 + (pltpu.VMEM((32, 384), BF),),
+        in_specs=[pl.BlockSpec(memory_space=pltpu.MemorySpace.HBM)] + [hbm] * 6,
+        out_specs=(vmem,) * 4,
+        scratch_shapes=[pltpu.SMEM((1,), jnp.int32)] + scratch + [
             pltpu.SemaphoreType.DMA((SEMS,)), pltpu.SemaphoreType.DMA((SEMS,)), pltpu.SemaphoreType.DMA((LOCALS,)),
         ],
         compiler_params=pltpu.CompilerParams(
@@ -525,13 +521,11 @@
     return pl.pallas_call(
         copy_out,
         out_shape=outs,
-        in_specs=[hbm] * 4,
-        out_specs=(hbm, hbm, hbm, vmem),
-        scratch_shapes=[
-            pltpu.VMEM((3, 128, 1536), BF), pltpu.VMEM((32, 384), BF), pltpu.SemaphoreType.DMA((13,)),
-        ],
+        in_specs=[vmem] * 4,
+        out_specs=(hbm,) * 4,
+        scratch_shapes=[pltpu.VMEM((6, 1536), F32), pltpu.SemaphoreType.DMA((4,))],
         name="copy_out",
-    )(*results)
+    )(*(pltpu.with_memory_space_constraint(r, pltpu.VMEM) for r in results))
 
 
 def solution(mesh):

time: 62.6 us -> 60.8 us (0.971)
  Pallas kernels: 61.2 us -> 59.4 us
    pallas_call x2, Pallas kernels: 61.2 us -> 59.4 us  [the longest x1 58.4 us: shards(): pl.pallas_call(kernel, out_shape=(pltpu.VMEM((128, 1536), BF),) * 3 + (pl...]
where the time goes in v5:
time: 60.8 us; the launch traced here: 60.7 us
  Pallas kernels  59.4 us (98%)
  between operations  1.29 us (2%)
    pallas_call x1, Pallas kernels, shards(): pl.pallas_call(kernel, out_shape=(pltpu.VMEM((128, 1536), BF),) * 3 + (pl...  58.4 us

profile of v5, /device:TPU:4, one launch (start us, length us, event | category | flops | bytes accessed | tf_op | source)
XLA Modules:
  0.0 60.7 jit_solution(10617329916758567930)
XLA Ops:
  1.3 58.4 %joint_attention_backward.1 = (bf16[128,1536]{1,0:T(8,128)(2,1)S(1)}, bf16[128,1536]{1,0:T(8,128)(2,1)S(1)}, bf16[128,1536]{1,0:T(8,128)(2,1)S(1)}, bf16[32,384]{1,0:T(8,128)(2,1)S(1)}) custom-call(s32[1]{0:T(128)S(6)} %copy.11.len_ref, bf16[128,1536]{1,0:T(8,128)(2,1)} %q_ref.1, bf16[128,1536]{1,0:T(8,128)(2,1)} %k_ref.1, bf16[128,1536]{1,0:T(8,128)(2,1)} %v_ref.1, ...), custom_call_target="tpu_custom_call" | custom-call | tf_op jit(solution)/shard_map/joint_attention_backward/pallas_call | solution.py:508
  59.7 1.0 %copy_out.1 = (bf16[128,1536]{1,0:T(8,128)(2,1)}, bf16[128,1536]{1,0:T(8,128)(2,1)}, bf16[128,1536]{1,0:T(8,128)(2,1)}, f32[6,1536]{1,0:T(8,128)}) custom-call(bf16[128,1536]{1,0:T(8,128)(2,1)S(1)} %get-tuple-element.8.gq, bf16[128,1536]{1,0:T(8,128)(2,1)S(1)} %get-tuple-element.9.gk, bf16[128,1536]{1,0:T(8,128)(2,1)S(1)} %get-tuple-element.10.gv, ...), custom_call_target="tpu_custom_call" | custom-call | tf_op jit(solution)/shard_map/copy_out/pallas_call | solution.py:521

commit v6 on v5

--- a/solution.py
+++ b/solution.py
@@ -13,7 +13,7 @@
 NT = (((1,), (1,)), ((), ()))
 TT = (((0,), (0,)), ((), ()))
 NN = (((1,), (0,)), ((), ()))
-SEMS, LOCALS = 44, 10
+SEMS, LOCALS = 42, 10
 
 
 def dot(a, b, dims):
@@ -227,8 +227,9 @@
         padded = jnp.concatenate([wz[i % 2, i // 2].astype(F32)[j * 8:(j + 1) * 8] for i in range(8)], axis=0).astype(BF)
         wbuf[c, x, :, j * 384:(j + 1) * 384] = dot(squeeze, padded, NN).astype(BF)
     quarter = wbuf.at[c, x]
-    wd_low = Group(quarter).send(quarter, quarter, at_x(x + 1))
-    wd_high = Group(quarter).send(quarter, quarter, at_x(x + 3))
+    wd = Group(wbuf.at[c, pl.ds(0, 3)])
+    for i in (2, 1, 3):
+        wd.send(quarter, quarter, at_x(x + i))
 
     def whole(buf, h, which):
         return buf[h, :, :, which].reshape(1024, 128)
@@ -258,13 +259,6 @@
     near_q[1].arrive()
     pass_q(1)
     forward(1)
-    wd_both = Group(quarter)
-    wd_low.arrive()
-    piece = wbuf.at[c, (x + 3) % 4, :, pl.ds(0, 768)]
-    wd_both.send(piece, piece, at_x(x + 1))
-    wd_high.arrive()
-    piece = wbuf.at[c, (x + 1) % 4, :, pl.ds(768, 768)]
-    wd_both.send(piece, piece, at_x(x + 3))
     from_low.arrive()
     from_both = Group(mine_d)
     piece = dbuf.at[(y + 3) % 4, pl.ds(16, 64)]
@@ -272,13 +266,29 @@
     from_high.arrive()
     piece = dbuf.at[(y + 1) % 4, pl.ds(80, 48)]
     from_both.send(piece, piece, at_y(y + 3))
-    wd_both.arrive()
+    wd.arrive()
     we = Group(wbuf.at[c]).send(wbuf.at[c], wbuf.at[c], mate_c)
     near_q[2].arrive()
     pass_q(2)
     forward(2)
     far_lse = Group(lse.at[1]).send(lse.at[0], lse.at[1], mate_z)
 
+    qi = lax.broadcasted_iota(jnp.int32, (384, 512), 1)
+    off = qi % 128
+    token = (zl * 4 + qi // 128) * 112 + off - 16
+    at_image = jnp.where((off >= 16) & (token < length), atbuf[...].astype(F32), 0.0)
+    at_image = at_image.astype(BF)
+
+    def features(half):
+        return dot(pick[half], at_image, NN).astype(BF)
+
+    halves = (slice(0, 768), slice(768, 1536))
+
+    def project(kept, out, part):
+        image = dbuf[:, :, part].reshape(512, 768)
+        out[:, :, part] = dot(kept, image, NN).astype(out.dtype).reshape(4, 48, 768)
+
+    kept_far, kept_own = features(1 - c), features(c)
     far_do = [Group(dob.at[h, 1]) for h in range(3)]
     caps.arrive()
     own_c.wait()
@@ -305,22 +315,6 @@
         for i in (0, 1, 3):
             pass_do(h, (y + i) % 4)
 
-    qi = lax.broadcasted_iota(jnp.int32, (384, 512), 1)
-    off = qi % 128
-    token = (zl * 4 + qi // 128) * 112 + off - 16
-    at_image = jnp.where((off >= 16) & (token < length), atbuf[...].astype(F32), 0.0)
-    at_image = at_image.astype(BF)
-
-    def features(half):
-        return dot(pick[half], at_image, NN).astype(BF)
-
-    halves = (slice(0, 768), slice(768, 1536))
-
-    def project(kept, out, part):
-        image = dbuf[:, :, part].reshape(512, 768)
-        out[:, :, part] = dot(kept, image, NN).astype(out.dtype).reshape(4, 48, 768)
-
-    kept_far, kept_own = features(1 - c), features(c)
     from_both.arrive()
 
     ge = []
@@ -378,6 +372,7 @@
         dkown[h] = dot(dsbuf[0:512], qb[0, :, :, lanes].reshape(512, 128), NN)
 
     def far_probs(h):
+        far_q[h].arrive()
         lanes = slice(h * 128, (h + 1) * 128)
         kk = kvb[h, 0, :, 0].reshape(512, 128)
         for t in range(2):
@@ -406,7 +401,6 @@
     backward(2)
     far_lse.arrive()
     for h in range(3):
-        far_q[h].arrive()
         far_probs(h)
     far_delta.arrive()
     far_backward(0)
@@ -430,8 +424,8 @@
 
     along_z(0)
     far_backward(1)
+    along_z(1)
     far_backward(2)
-    along_z(1)
 
     for group in gc:
         group.arrive()

time: 60.8 us -> 59.4 us (0.977)
  Pallas kernels: 59.4 us -> 58.1 us
    pallas_call x1, Pallas kernels: 58.4 us -> 57 us  [shards(): pl.pallas_call(kernel, out_shape=(pltpu.VMEM((128, 1536), BF),) * 3 + (pl...]
where the time goes in v6:
time: 59.4 us
  Pallas kernels  58.1 us (98%)
  between operations  1.29 us (2%)
    pallas_call x1, Pallas kernels, shards(): pl.pallas_call(kernel, out_shape=(pltpu.VMEM((128, 1536), BF),) * 3 + (pl...  57 us

profile of v6, /device:TPU:4, one launch (start us, length us, event | category | flops | bytes accessed | tf_op | source)
XLA Modules:
  0.0 59.4 jit_solution(11288147376587281709)
XLA Ops:
  1.3 57.0 %joint_attention_backward.1 = (bf16[128,1536]{1,0:T(8,128)(2,1)S(1)}, bf16[128,1536]{1,0:T(8,128)(2,1)S(1)}, bf16[128,1536]{1,0:T(8,128)(2,1)S(1)}, bf16[32,384]{1,0:T(8,128)(2,1)S(1)}) custom-call(s32[1]{0:T(128)S(6)} %copy.11.len_ref, bf16[128,1536]{1,0:T(8,128)(2,1)} %q_ref.1, bf16[128,1536]{1,0:T(8,128)(2,1)} %k_ref.1, bf16[128,1536]{1,0:T(8,128)(2,1)} %v_ref.1, ...), custom_call_target="tpu_custom_call" | custom-call | tf_op jit(solution)/shard_map/joint_attention_backward/pallas_call | solution.py:502
  58.3 1.0 %copy_out.1 = (bf16[128,1536]{1,0:T(8,128)(2,1)}, bf16[128,1536]{1,0:T(8,128)(2,1)}, bf16[128,1536]{1,0:T(8,128)(2,1)}, f32[6,1536]{1,0:T(8,128)}) custom-call(bf16[128,1536]{1,0:T(8,128)(2,1)S(1)} %get-tuple-element.8.gq, bf16[128,1536]{1,0:T(8,128)(2,1)S(1)} %get-tuple-element.9.gk, bf16[128,1536]{1,0:T(8,128)(2,1)S(1)} %get-tuple-element.10.gv, ...), custom_call_target="tpu_custom_call" | custom-call | tf_op jit(solution)/shard_map/copy_out/pallas_call | solution.py:515

commit v7 on v6

--- a/solution.py
+++ b/solution.py
@@ -13,7 +13,7 @@
 NT = (((1,), (1,)), ((), ()))
 TT = (((0,), (0,)), ((), ()))
 NN = (((1,), (0,)), ((), ()))
-SEMS, LOCALS = 42, 10
+SEMS, SEND_SEMS, LOCALS = 42, 19, 10
 
 
 def dot(a, b, dims):
@@ -51,33 +51,40 @@
     zh = z // 2
     on_diagonal = x == y
     off_diagonal = x != y
-    count = [0]
-    groups = []
+    count = [0, 0]
+    pools = []
+
+    def whole_copy(bulk, send_slot, recv_slot):
+        return pltpu.make_async_remote_copy(
+            src_ref=bulk, dst_ref=bulk, send_sem=ssem.at[send_slot], recv_sem=rsem.at[recv_slot],
+            device_id=mate_c, device_id_type=MESH,
+        )
+
+    class Pool:
+        def __init__(self, bulk, kept=True):
+            self.slot, self.bulk = count[1], bulk
+            count[1] += 1
+            if kept:
+                pools.append(self)
+
+        def leave(self):
+            whole_copy(self.bulk, self.slot, 0).wait_send()
 
     class Group:
-        def __init__(self, bulk):
+        def __init__(self, bulk, pool=None):
             self.slot, self.bulk = count[0], bulk
+            self.pool = pool or Pool(bulk)
             count[0] += 1
-            groups.append(self)
 
         def send(self, src, dst, to):
             pltpu.make_async_remote_copy(
-                src_ref=src, dst_ref=dst, send_sem=ssem.at[self.slot], recv_sem=rsem.at[self.slot],
+                src_ref=src, dst_ref=dst, send_sem=ssem.at[self.pool.slot], recv_sem=rsem.at[self.slot],
                 device_id=to, device_id_type=MESH,
             ).start()
             return self
 
-        def whole(self, bulk):
-            return pltpu.make_async_remote_copy(
-                src_ref=bulk, dst_ref=bulk, send_sem=ssem.at[self.slot], recv_sem=rsem.at[self.slot],
-                device_id=mate_c, device_id_type=MESH,
-            )
-
         def arrive(self):
-            self.whole(self.bulk).wait_recv()
-
-        def leave(self):
-            self.whole(self.bulk).wait_send()
+            whole_copy(self.bulk, self.pool.slot, self.slot).wait_recv()
 
     def at_x(xx):
         return device(xx % 4, y, z, c)
@@ -131,7 +138,7 @@
     own_w.wait()
     w = jnp.concatenate([wbuf6[...].astype(F32), jnp.zeros((2, 1536), F32)], axis=0)
     wsend[...] = jnp.concatenate([w[:, j * 384:(j + 1) * 384] for j in range(4)], axis=0).astype(BF)
-    wa = Group(wz.at[0, 0])
+    wa = Group(wz.at[0, 0], Pool(wz.at[0, 0], False))
 
     @pl.when(off_diagonal)
     def _():
@@ -142,18 +149,21 @@
         wz[zl, zh] = wsend[...]
 
     came = [[] for _ in range(3)]
+    kv_out, far_out = Pool(kvb.at[:, 0, pl.ds(0, 3)]), Pool(kvb)
+    q_out, image_out = Pool(qb.at[0, pl.ds(0, 3)]), Pool(dbuf.at[pl.ds(0, 3), pl.ds(16, 112)])
+    stat_out, grad_out = Pool(lse), Pool(low2buf.at[:, pl.ds(0, 288)])
 
     def exchange(h):
         for i in (1, 3, 2):
             lane = cols((y + i) % 4 * 3 + h, 128)
             source = (y + 4 - i) % 4
-            g = Group(kvb.at[h, 0, source])
+            g = Group(kvb.at[h, 0, source], kv_out)
             g.send(k_ref.at[:, lane], kvb.at[h, 0, y, 0], at_y(y + i))
             g.send(v_ref.at[:, lane], kvb.at[h, 0, y, 1], at_y(y + i))
             came[h].append((source, g))
 
-    far_kv = [Group(kvb.at[h, 1]) for h in range(3)]
-    far_q = [Group(qb.at[1, :, :, pl.ds(h * 128, 128)]) for h in range(3)]
+    far_kv = [Group(kvb.at[h, 1], far_out) for h in range(3)]
+    far_q = [Group(qb.at[1, :, :, pl.ds(h * 128, 128)], far_out) for h in range(3)]
 
     def pass_kv(h, p):
         far_kv[h].send(kvb.at[h, 0, p], kvb.at[h, 1, p], mate_z)
@@ -164,9 +174,9 @@
             p = (y + i) % 4
             far_q[h].send(qb.at[0, p, :, lane], qb.at[1, p, :, lane], mate_z)
 
-    near_q = [Group(qb.at[0, pl.ds(0, 3), :, pl.ds(h * 128, 128)]) for h in range(3)]
+    near_q = [Group(qb.at[0, pl.ds(0, 3), :, pl.ds(h * 128, 128)], q_out) for h in range(3)]
     mine_d = dbuf.at[y, pl.ds(16, 112)]
-    from_low, from_high = Group(mine_d), Group(mine_d)
+    from_low, from_high = Group(mine_d, image_out), Group(mine_d, image_out)
 
     def exchange_q(h):
         for i in (1, 3, 2):
@@ -260,7 +270,7 @@
     pass_q(1)
     forward(1)
     from_low.arrive()
-    from_both = Group(mine_d)
+    from_both = Group(mine_d, image_out)
     piece = dbuf.at[(y + 3) % 4, pl.ds(16, 64)]
     from_both.send(piece, piece, at_y(y + 1))
     from_high.arrive()
@@ -271,7 +281,7 @@
     near_q[2].arrive()
     pass_q(2)
     forward(2)
-    far_lse = Group(lse.at[1]).send(lse.at[0], lse.at[1], mate_z)
+    far_lse = Group(lse.at[1], stat_out).send(lse.at[0], lse.at[1], mate_z)
 
     qi = lax.broadcasted_iota(jnp.int32, (384, 512), 1)
     off = qi % 128
@@ -289,7 +299,7 @@
         out[:, :, part] = dot(kept, image, NN).astype(out.dtype).reshape(4, 48, 768)
 
     kept_far, kept_own = features(1 - c), features(c)
-    far_do = [Group(dob.at[h, 1]) for h in range(3)]
+    far_do = [Group(dob.at[h, 1], far_out) for h in range(3)]
     caps.arrive()
     own_c.wait()
     we.arrive()
@@ -345,12 +355,12 @@
             delta[0, h:h + 1, part] = jnp.sum(
                 do.astype(F32).T * atbuf[lanes, part].astype(F32), axis=0, keepdims=True
             )
-    far_delta = Group(delta.at[1]).send(delta.at[0], delta.at[1], mate_z)
+    far_delta = Group(delta.at[1], stat_out).send(delta.at[0], delta.at[1], mate_z)
     for h in range(2):
         pass_do(h, (y + 2) % 4)
     far_do[2].send(dob.at[2, 0], dob.at[2, 1], mate_z)
 
-    outs = [(Group(ref.at[:, pl.ds(0, 1152)]), ref, 4 + i) for i, ref in enumerate((gq_ref, gk_ref, gv_ref))]
+    outs = [(Group(ref.at[:, pl.ds(0, 1152)], grad_out), ref, 4 + i) for i, ref in enumerate((gq_ref, gk_ref, gv_ref))]
 
     def to_rows(src, which, h):
         group, out, sem = outs[which]
@@ -434,7 +444,7 @@
         total += crecv[i].astype(F32)
     total = total.reshape(32, 384)
     asend[...] = total.astype(BF)
-    ga = Group(gp_ref)
+    ga = Group(gp_ref, Pool(gp_ref, False))
 
     @pl.when(off_diagonal)
     def _():
@@ -448,21 +458,20 @@
         group.arrive()
         bulk = out.at[:, pl.ds(0, 384)]
         pltpu.make_async_copy(bulk, bulk, lsem.at[sem]).wait()
-    for group in groups:
-        if group not in (wa, ga):
-            group.leave()
+    for pool in pools:
+        pool.leave()
 
     @pl.when(off_diagonal)
     def _():
-        wa.leave()
-        ga.leave()
+        wa.pool.leave()
+        ga.pool.leave()
         ga.arrive()
 
     @pl.when(on_diagonal)
     def _():
         pltpu.make_async_copy(asend, gp_ref, lsem.at[8]).wait()
 
-    assert count[0] == SEMS
+    assert count == [SEMS, SEND_SEMS]
 
 
 def copy_out(gq, gk, gv, gp, gq_out, gk_out, gv_out, gp_out, gp_buf, sem):
@@ -505,7 +514,7 @@
         in_specs=[pl.BlockSpec(memory_space=pltpu.MemorySpace.HBM)] + [hbm] * 6,
         out_specs=(vmem,) * 4,
         scratch_shapes=[pltpu.SMEM((1,), jnp.int32)] + scratch + [
-            pltpu.SemaphoreType.DMA((SEMS,)), pltpu.SemaphoreType.DMA((SEMS,)), pltpu.SemaphoreType.DMA((LOCALS,)),
+            pltpu.SemaphoreType.DMA((SEND_SEMS,)), pltpu.SemaphoreType.DMA((SEMS,)), pltpu.SemaphoreType.DMA((LOCALS,)),
         ],
         compiler_params=pltpu.CompilerParams(
             collective_id=0, has_side_effects=True, vmem_limit_bytes=56 * 2**20

time: 59.4 us -> 59.2 us (level)
  no operation moved by 1% of the time
where the time goes in v7:
time: 59.2 us; the launch traced here: 59.1 us
  Pallas kernels  57.9 us (98%)
  between operations  1.29 us (2%)
    pallas_call x1, Pallas kernels, shards(): pl.pallas_call(kernel, out_shape=(pltpu.VMEM((128, 1536), BF),) * 3 + (pl...  56.8 us

profile of v7, /device:TPU:4, one launch (start us, length us, event | category | flops | bytes accessed | tf_op | source)
XLA Modules:
  0.0 59.1 jit_solution(15466589064539817557)
XLA Ops:
  1.3 56.8 %joint_attention_backward.1 = (bf16[128,1536]{1,0:T(8,128)(2,1)S(1)}, bf16[128,1536]{1,0:T(8,128)(2,1)S(1)}, bf16[128,1536]{1,0:T(8,128)(2,1)S(1)}, bf16[32,384]{1,0:T(8,128)(2,1)S(1)}) custom-call(s32[1]{0:T(128)S(6)} %copy.11.len_ref, bf16[128,1536]{1,0:T(8,128)(2,1)} %q_ref.1, bf16[128,1536]{1,0:T(8,128)(2,1)} %k_ref.1, bf16[128,1536]{1,0:T(8,128)(2,1)} %v_ref.1, ...), custom_call_target="tpu_custom_call" | custom-call | tf_op jit(solution)/shard_map/joint_attention_backward/pallas_call | solution.py:511
  58.1 1.0 %copy_out.1 = (bf16[128,1536]{1,0:T(8,128)(2,1)}, bf16[128,1536]{1,0:T(8,128)(2,1)}, bf16[128,1536]{1,0:T(8,128)(2,1)}, f32[6,1536]{1,0:T(8,128)}) custom-call(bf16[128,1536]{1,0:T(8,128)(2,1)S(1)} %get-tuple-element.8.gq, bf16[128,1536]{1,0:T(8,128)(2,1)S(1)} %get-tuple-element.9.gk, bf16[128,1536]{1,0:T(8,128)(2,1)S(1)} %get-tuple-element.10.gv, ...), custom_call_target="tpu_custom_call" | custom-call | tf_op jit(solution)/shard_map/copy_out/pallas_call | solution.py:524
